TPU v7x, 32 devices: a whole 2x2x4 slice. The times are simulated.
32 devices in a mesh: grp: 2 (over y), seq: 4 (over z), head: 4 (over x, core).
Axes of the slice: x: 2, y: 2, z: 4, core: 2. Of those that a mesh axis runs over, the one named last changes fastest.
Arguments:
- q_heads: bfloat16 [8, 64, 16384], P('head', None, ('grp', 'seq')), parts along dimension 2, may hold values from -12 to 12
- k_heads: bfloat16 [8, 64, 16384], P('head', None, ('grp', 'seq')), parts along dimension 2, may hold values from -10 to 10
- v_heads: bfloat16 [8, 64, 16384], P('head', None, ('grp', 'seq')), parts along dimension 2, may hold values from -10 to 10
- morton_order: int32 [8, 2048], P(('grp', 'seq')), parts along dimension 0, may hold values from 0 to 2047, each once within a row
- leaf_counts: int32 [64], P('grp'), parts along dimension 0, may hold values from 64 to 256, as said below
Outputs:
- attended: bfloat16 [8, 64, 16384], P('head', None, ('grp', 'seq')), parts along dimension 2
There are 2 independent parts, one for each index of `grp`. A program takes and returns all parts, laid end to end along the dimension named above; each array names one. Nothing has to cross between parts.
Inputs may be any that keep to these rules, and one draw needn't show every extreme that they name: `morton_order`: each row holds every number of 0 .. 2047 once. `leaf_counts`: the valid points of a leaf are its first ones.
All inputs are finite; a program needn't handle non-finite values.
Results may differ from a plain program's by a relative error of at most 0.0021.
Values may be sent and summed in bfloat16 or wider, within the bound.
No kernel may reach another device: no remote copies, remote signals or barrier semaphores. Data moves between devices by JAX's collectives and lax.ppermute only.
A program may use at most 64 MiB of HBM per device.

v0:
```python
import functools
import math

import jax
import jax.numpy as jnp
from jax import lax
from jax.experimental import pallas as pl
from jax.experimental.pallas import tpu as pltpu
from jax.sharding import PartitionSpec as P

LEAF = 256
HEAD = 64
LANES = 128
MASKED = -1e30
F32 = jnp.float32
BF16 = jnp.bfloat16
SCALE = math.log2(math.e) / math.sqrt(HEAD)
SENT = BF16
TERMS = 2


def dot(a, b):
    return lax.dot_general(a, b, (((1,), (0,)), ((), ())), preferred_element_type=F32)


def iota(shape, dim):
    return lax.broadcasted_iota(jnp.int32, shape, dim)


def bits(cond):
    return jnp.where(cond, 1.0, 0.0).astype(BF16)


def split(x, terms=2):
    out = []
    for _ in range(terms - 1):
        out.append(x.astype(BF16))
        x = x - out[-1].astype(F32)
    return out + [x.astype(BF16)]


def encode(x):
    return split(x, TERMS)


def decode(terms):
    return functools.reduce(jnp.add, [t.astype(F32) for t in terms])


def one_hot(order_row, tokens):
    high = order_row // LEAF
    low = (order_row - high * LEAF).astype(F32).astype(BF16)
    slots = iota((LEAF, LEAF), 0).astype(F32).astype(BF16)
    base = jnp.where(slots == low, jnp.ones((), BF16), jnp.zeros((), BF16))
    return jnp.concatenate([base * bits(high == j) for j in range(tokens // LEAF)], axis=0)


def pool_matrix(group, first_row, rows):
    return bits(iota((LEAF, rows), 0) // group + first_row == iota((LEAF, rows), 1))


def pool_rows(group, first_row, rows):
    return bits(iota((rows, LEAF), 1) // group + first_row == iota((rows, LEAF), 0))


def level_shape(level, tokens):
    group = 2**level
    rows = tokens // group
    return group, max(min(rows, LEAF), LANES), max(rows // LEAF, 1)


def place(level, leaf, tokens):
    group, rows, _ = level_shape(level, tokens)
    per_leaf = LEAF // group
    return (leaf * per_leaf) // rows, (leaf * per_leaf) % rows


def pooled_cols(level, leaf_values, tokens):
    group, rows, blocks = level_shape(level, tokens)
    sums = [None] * blocks
    for leaf, values in enumerate(leaf_values):
        block, first = place(level, leaf, tokens)
        if LEAF // group == LANES:
            piece = dot(values, pool_matrix(group, 0, LANES))
            old = sums[block]
            sums[block] = piece if old is None else jnp.concatenate([old, piece], axis=1)
        else:
            piece = dot(values, pool_matrix(group, first, rows))
            sums[block] = piece if sums[block] is None else sums[block] + piece
    return sums


def pooled_rows(level, leaf_values, tokens):
    group, rows, blocks = level_shape(level, tokens)
    per_leaf = LEAF // group
    sums = [None] * blocks
    for leaf, values in enumerate(leaf_values):
        block, first = place(level, leaf, tokens)
        old = sums[block]
        if per_leaf % 16 == 0:
            piece = dot(pool_rows(group, 0, per_leaf), values)
            sums[block] = piece if old is None else jnp.concatenate([old, piece], axis=0)
        else:
            piece = dot(pool_rows(group, first, rows), values)
            sums[block] = piece if old is None else old + piece
    return sums


def mass(counts, first_leaf, leaves, group, shape, dim):
    row = iota(shape, dim)
    per_leaf = LEAF // group
    leaf = row // per_leaf
    held = jnp.zeros(shape, jnp.int32)
    for n in range(leaves):
        held = jnp.where(leaf == n, counts[first_leaf + n], held)
    return jnp.clip(held - (row % per_leaf) * group, 0, group)


def near_marks(empty):
    return jnp.where((iota(empty.shape, 1) == 0) & empty, MASKED, 0.0).astype(BF16)


def far_marks(empty):
    return jnp.where((iota(empty.shape, 1) == HEAD) & empty, MASKED, 0.0)


def by_head(both):
    turned = pltpu.roll(both, HEAD, 1)
    return (both, turned), (turned, both)


def far_keys(means, mark):
    hi, lo = split(means)
    hi_left, _ = by_head(hi.astype(F32))
    _, lo_right = by_head(lo.astype(F32))
    lane = iota(mark.shape, 1) < HEAD
    out = []
    for h in range(2):
        both = jnp.where(lane, hi_left[h], lo_right[h]).astype(BF16)
        once = jnp.where(lane, hi_left[h], mark).astype(BF16)
        out.append(jnp.concatenate([both, once], axis=1))
    return out


def far_values(sums, mass_rows):
    hi, lo = split(sums.T)
    return [
        jnp.concatenate([hi[h * HEAD : (h + 1) * HEAD], lo[h * HEAD : (h + 1) * HEAD], mass_rows], axis=0)
        for h in range(2)
    ]


def near_scores(k_window, mark, query):
    none = jnp.zeros((HEAD, LEAF), BF16)
    right = jnp.concatenate(
        [
            jnp.concatenate([query[:HEAD], none], axis=1),
            jnp.concatenate([none, query[HEAD:]], axis=1),
            bits(iota((LANES, 2 * LEAF), 0) == 0),
        ],
        axis=0,
    )
    left = jnp.concatenate([k_window, mark], axis=1)
    return [dot(left[i * LEAF : (i + 1) * LEAF], right) for i in range(3)]


def near(scores, v_window, h):
    scores = [piece[:, h * LEAF : (h + 1) * LEAF] for piece in scores]
    top = functools.reduce(jnp.maximum, [jnp.max(x, axis=0, keepdims=True) for x in scores])
    sums = totals = 0.0
    for i, piece in enumerate(scores):
        weights = jnp.exp2((piece - top) * SCALE)
        totals = totals + jnp.sum(weights, axis=0, keepdims=True)
        value = v_window[h * HEAD : (h + 1) * HEAD, i * LEAF : (i + 1) * LEAF]
        sums = sums + dot(value, weights.astype(BF16))
    return top * SCALE, sums, totals


def far_scores(keys, query):
    hi, lo = query[:HEAD], query[HEAD:]
    flag = bits(iota((HEAD, query.shape[1]), 0) == 0)
    return dot(keys, jnp.concatenate([hi, hi, lo, flag], axis=0))


def far(scores, value):
    top = jnp.max(scores, axis=0, keepdims=True).astype(BF16).astype(F32)
    w_hi, w_lo = split(jnp.exp2(scores - top))
    out = dot(jnp.concatenate([value, value], axis=1), jnp.concatenate([w_hi, w_lo], axis=0))
    return top, out[:HEAD] + out[HEAD : 2 * HEAD], out[2 * HEAD : 2 * HEAD + 1]


def staggered(units):
    held = None
    for first, second in units:
        scores = first()
        if held is not None:
            held[0](held[1])
        held = (second, scores)
    held[0](held[1])


def to_spread(term):
    top, sums, totals = term
    row = iota((16, sums.shape[1]), 0)
    t_hi, t_lo = split(totals)
    tail = jnp.where(row == 0, t_hi.astype(F32), jnp.where(row == 1, t_lo.astype(F32), top))
    hi, lo = split(sums)
    return jnp.concatenate([hi, lo, tail.astype(BF16)], axis=0)


def spread(rows, times, first, width):
    size = (rows.shape[1], width)
    x = dot(rows, bits(iota(size, 0) == iota(size, 1) // times + first))
    tail = x[2 * HEAD :]
    return tail[2:3], x[:HEAD] + x[HEAD : 2 * HEAD], tail[0:1] + tail[1:2]


def merge(terms):
    top = functools.reduce(jnp.maximum, [t[0] for t in terms])
    sums = totals = 0.0
    for t in terms:
        factor = jnp.exp2(t[0] - top)
        sums = sums + t[1] * factor
        totals = totals + t[2] * factor
    return top, sums, totals


def halo_rows():
    return 2 * LEAF


def pack_rows(index, tokens, level):
    rows = 2 * TERMS * level_shape(level, tokens)[1]
    return rows + (halo_rows() if index == 0 else 0)


def kv_kernel(
    tokens, remote, counts_in, order_in, k_in, v_in, kv_rows, v_cols, order, *rest
):
    packs, (counts, k, v, sems) = rest[: len(remote) + 1], rest[len(remote) + 1 :]
    copies = [
        pltpu.make_async_copy(source, target, sems.at[i])
        for i, (source, target) in enumerate(
            ((order_in, order), (k_in, k), (v_in, v), (counts_in, counts))
        )
    ]
    for copy in copies:
        copy.start()
    for copy in copies:
        copy.wait()
    rank = lax.axis_index("seq")
    leaves = tokens // LEAF
    joint = jnp.concatenate([k[...], v[...]], axis=0)
    masked = []
    for n in range(leaves):
        cols = slice(n * LEAF, (n + 1) * LEAF)
        got = dot(joint, one_hot(order[:, cols], tokens)).astype(BF16)
        rows = got.T
        kv_rows[cols, :] = rows
        v_cols[:, cols] = got[LANES:]
        held = iota((LEAF, 2 * LANES), 0) < counts[rank * leaves + n]
        masked.append(jnp.where(held, rows.astype(F32), 0.0).astype(BF16))
    odd = rank % 2 == 1
    pair, step = packs[:2]

    def halo(ref, leaf):
        rows = slice(leaf * LEAF, (leaf + 1) * LEAF)
        ref[0:LEAF, :] = kv_rows[rows, :LANES]
        for half in range(2):
            at = leaf * LEAF + half * LANES
            ref[LEAF + half * LANES : LEAF + (half + 1) * LANES, :] = v_cols[:, at : at + LANES]

    @pl.when(odd)
    def _():
        halo(pair, 0)
        halo(step, leaves - 1)

    @pl.when(jnp.logical_not(odd))
    def _():
        halo(pair, leaves - 1)
        halo(step, 0)

    for index, level in enumerate(remote):
        ref = pair if index == 0 else packs[index + 1]
        at = halo_rows() if index == 0 else 0
        group, rows, _ = level_shape(level, tokens)
        (sums,) = pooled_rows(level, masked, tokens)
        weight = mass(counts, rank * leaves, leaves, group, (rows, LANES), 0).astype(F32)
        means = sums[:, :LANES] / jnp.maximum(weight, 1.0)
        for term in encode(means) + encode(sums[:, LANES:] * (1.0 / group)):
            ref[at : at + rows, :] = term
            at += rows


def local_kernel(tokens, remote, counts_in, q, order, kv_rows, v_cols, *rest):
    levels = len(remote)
    near_out, near_stat, far_out, far_stat, q_ends, end_marks = rest[:6]
    rest = rest[6:]
    queries_out, marks_out, mass_out = rest[:levels], rest[levels : 2 * levels], rest[2 * levels : 3 * levels]
    counts, sem, mark = rest[3 * levels :]
    copy = pltpu.make_async_copy(counts_in, counts, sem)
    copy.start()
    rank = lax.axis_index("seq")
    count = lax.axis_size("seq")
    leaves = tokens // LEAF
    first_leaf = rank * leaves
    joint = q[...]
    copy.wait()
    masked = []
    for n in range(leaves):
        rows = slice(n * LEAF, (n + 1) * LEAF)
        mark[rows, :] = near_marks(iota((LEAF, LANES), 0) >= counts[first_leaf + n])
        held = iota((LEAF, 2 * LANES), 0) < counts[first_leaf + n]
        masked.append(jnp.where(held, kv_rows[rows, :].astype(F32), 0.0).astype(BF16))
    leaf_q = [None] * leaves

    def gather(n):
        cols = slice(n * LEAF, (n + 1) * LEAF)
        leaf_q[n] = dot(joint, one_hot(order[:, cols], tokens)).astype(BF16)

    def near_unit(n):
        cols = slice(n * LEAF, (n + 1) * LEAF)
        window = slice((n - 1) * LEAF, (n + 2) * LEAF)

        def first():
            gather(n)
            return near_scores(kv_rows[window, :LANES], mark[window, :], leaf_q[n])

        def second(scores):
            for h in range(2):
                top, sums, totals = near(scores, v_cols[:, window], h)
                near_out[h, :, cols] = sums
                near_stat[h, 0:1, cols] = top
                near_stat[h, 1:2, cols] = totals

        return first, second

    gather(0)
    gather(leaves - 1)
    staggered([near_unit(n) for n in range(1, leaves - 1)])
    q_ends[:, :LEAF] = leaf_q[0]
    q_ends[:, LEAF:] = leaf_q[-1]

    def queries(level):
        out = []
        for sums in pooled_cols(level, leaf_q, tokens):
            hi, lo = split(sums * (SCALE / 2**level))
            out.append(
                [
                    jnp.concatenate([x[h * HEAD : (h + 1) * HEAD] for x in (hi, lo)], axis=0)
                    for h in range(2)
                ]
            )
        return out

    for index, level in enumerate(remote):
        (block,) = queries(level)
        for h in range(2):
            queries_out[index][h] = block[h]

    results = {}
    units = []
    for level in (2, 1):
        group, rows, blocks = level_shape(level, tokens)
        per_block = rows * group // LEAF
        level_queries = queries(level)
        for block, sums in enumerate(pooled_rows(level, masked, tokens)):
            start = first_leaf + block * per_block
            weight = mass(counts, start, per_block, group, (rows, LANES), 0)
            lanes = mass(counts, start, per_block, group, (16, rows), 1)
            keys = far_keys(
                sums[:, :LANES] / jnp.maximum(weight.astype(F32), 1.0), far_marks(weight == 0)
            )
            values = far_values(sums[:, LANES:], lanes.astype(F32).astype(BF16))
            for h in range(2):
                query = level_queries[block ^ 1][h]

                def second(scores, at=(level, block ^ 1, h), value=values[h]):
                    results[at] = far(scores, value)

                units.append((functools.partial(far_scores, keys[h], query), second))
    staggered(units)
    for block in range(level_shape(1, tokens)[2]):
        cols = slice(block * LEAF, (block + 1) * LEAF)
        for h in range(2):
            coarse = to_spread(results[2, block // 2, h])
            top, sums, totals = merge(
                [results[1, block, h], spread(coarse, 2, (block % 2) * LANES, LEAF)]
            )
            far_out[h, :, cols] = sums
            far_stat[h, 0:1, cols] = top
            far_stat[h, 1:2, cols] = totals

    for side, leaf in ((0, first_leaf - 1), (1, first_leaf + leaves)):
        there = jnp.logical_and(leaf >= 0, leaf < count * leaves)
        held = jnp.where(there, counts[jnp.clip(leaf, 0, count * leaves - 1)], 0)
        end_marks[side, :LEAF] = near_marks(iota((LEAF, LANES), 0) >= held)
        inner = side * (leaves - 2) * LEAF
        end_marks[side, LEAF:] = mark[inner : inner + 2 * LEAF, :]
    for index, level in enumerate(remote):
        group, rows, _ = level_shape(level, tokens)
        for i in range(2**index):
            start = (rank ^ (2**index + i)) * leaves
            at = slice(i * rows, (i + 1) * rows)
            weight = mass(counts, start, leaves, group, (rows, LANES), 0)
            marks_out[index][at, :] = far_marks(weight == 0)
            lanes = mass(counts, start, leaves, group, (16, rows), 1)
            mass_out[index][:, at] = lanes.astype(F32).astype(BF16)


def last_kernel(
    tokens, remote, near_in, near_stat, far_in, far_stat, q_ends, end_marks, kv_rows, v_cols, *rest
):
    levels = len(remote)
    queries, marks_in, mass_in = rest[:levels], rest[levels : 2 * levels], rest[2 * levels : 3 * levels]
    pair, step = rest[3 * levels : 3 * levels + 2]
    packs = rest[3 * levels + 2 : -3]
    out, stage, sems = rest[-3:]
    rank = lax.axis_index("seq")
    leaves = tokens // LEAF
    flag = jnp.where(rank % 2 == 1, 1, 0)
    ends = {}
    results = {}

    def near_unit(side):
        own = flag if side == 0 else 1 - flag
        inner = slice(side * (leaves - 2) * LEAF, (side * (leaves - 2) + 2) * LEAF)

        def chosen(at):
            here = pair[at, :].astype(F32)
            there = step[at, :].astype(F32)
            return jnp.where(own == 1, here, there).astype(BF16)

        def first():
            return near_scores(
                jnp.concatenate([chosen(slice(0, LEAF)), kv_rows[inner, :LANES]], axis=0),
                end_marks[side],
                q_ends[:, side * LEAF : (side + 1) * LEAF],
            )

        def second(scores):
            halves = [chosen(slice(LEAF + i * LANES, LEAF + (i + 1) * LANES)) for i in range(2)]
            window = jnp.concatenate(halves + [v_cols[:, inner]], axis=1)
            for h in range(2):
                ends[side * (leaves - 1), h] = near(scores, window, h)

        return first, second

    def far_units(index):
        level = remote[index]
        group, rows, _ = level_shape(level, tokens)
        fields = [[], []]
        for i in range(2**index):
            ref = pair if index == 0 else packs[2**index - 2 + i]
            at = halo_rows() if index == 0 else 0
            for field in fields:
                field.append(decode([ref[at + t * rows : at + (t + 1) * rows, :] for t in range(TERMS)]))
                at += TERMS * rows
        means, sums = [jnp.concatenate(field, axis=0) for field in fields]
        keys = far_keys(means, marks_in[index][...])
        values = far_values(sums * group, mass_in[index][...])
        units = []
        for h in range(2):

            def second(scores, h=h):
                results[index, h] = far(scores, values[h])

            units.append((functools.partial(far_scores, keys[h], queries[index][h]), second))
        return units

    units = [near_unit(0), near_unit(1)]
    for index in range(levels):
        units += far_units(index)
    staggered(units)

    coarse = []
    for h in range(2):
        merged = results[levels - 1, h]
        for index in reversed(range(levels - 1)):
            rows = level_shape(remote[index], tokens)[1]
            merged = merge([results[index, h], spread(to_spread(merged), 2, 0, rows)])
        coarse.append(to_spread(merged))
    step_rows = LEAF // 2 ** (remote[0] - 1)
    copies = []
    for block in range(leaves // 2):
        far_cols = slice(block * LEAF, (block + 1) * LEAF)
        for h in range(2):
            far_term = merge(
                [
                    (far_stat[h, 0:1, far_cols], far_in[h, :, far_cols], far_stat[h, 1:2, far_cols]),
                    spread(coarse[h], 2 ** (remote[0] - 1), block * step_rows, LEAF),
                ]
            )
            fine = to_spread(far_term)
            for part in range(2):
                n = 2 * block + part
                cols = slice(n * LEAF, (n + 1) * LEAF)
                if (n, h) in ends:
                    near_term = ends[n, h]
                else:
                    near_term = (near_stat[h, 0:1, cols], near_in[h, :, cols], near_stat[h, 1:2, cols])
                _, sums, totals = merge([near_term, spread(fine, 2, part * LANES, LEAF)])
                stage[h, :, cols] = (sums / totals).astype(BF16)
        cols = slice(2 * block * LEAF, 2 * (block + 1) * LEAF)
        copies.append(
            pltpu.make_async_copy(stage.at[:, :, cols], out.at[:, :, cols], sems.at[block])
        )
        copies[-1].start()
    for copy in copies:
        copy.wait()


VMEM = pl.BlockSpec(memory_space=pltpu.VMEM)
HBM = pl.BlockSpec(memory_space=pl.ANY)


def params():
    return pltpu.CompilerParams(vmem_limit_bytes=48 * 2**20)


def head_pair(q, k, v, order, counts):
    tokens = q.shape[2]
    leaves = tokens // LEAF
    count = lax.axis_size("seq")
    depth = (tokens * count // LEAF).bit_length() - 1
    remote = tuple(range(leaves.bit_length() - 1, depth))
    flat = (2 * HEAD, tokens)
    shape = jax.ShapeDtypeStruct
    outs = [
        shape((tokens, 4 * HEAD), BF16),
        shape(flat, BF16),
        shape((1, tokens), jnp.int32),
        shape((pack_rows(0, tokens, remote[0]), LANES), SENT),
        shape((halo_rows(), LANES), SENT),
    ] + [shape((pack_rows(i, tokens, remote[i]), LANES), SENT) for i in range(1, len(remote))]
    made = pl.pallas_call(
        functools.partial(kv_kernel, tokens, remote),
        out_shape=outs,
        in_specs=[HBM] * 4,
        out_specs=[VMEM] * len(outs),
        scratch_shapes=[
            pltpu.SMEM(counts.shape, jnp.int32),
            pltpu.VMEM(flat, BF16),
            pltpu.VMEM(flat, BF16),
            pltpu.SemaphoreType.DMA((4,)),
        ],
        compiler_params=params(),
        cost_estimate=pl.CostEstimate(
            flops=2 * 256 * tokens * tokens, bytes_accessed=4 * 2**20, transcendentals=0
        ),
        name="gather_keys",
    )(*(pltpu.with_memory_space_constraint(x, pltpu.HBM) for x in (counts, order, k.reshape(flat), v.reshape(flat))))
    kv_rows, v_cols, order_here, pair, step = made[:5]
    packs = made[5:]

    got_pair = lax.ppermute(pair, "seq", [(i, i ^ 1) for i in range(count)])
    swaps = []
    for i in range(1, count - 1, 2):
        swaps += [(i, i + 1), (i + 1, i)]
    got_step = lax.ppermute(step, "seq", swaps) if swaps else jnp.zeros_like(step)
    got = []
    for index in range(1, len(remote)):
        for partner in range(2**index, 2 ** (index + 1)):
            got.append(
                lax.ppermute(packs[index - 1], "seq", [(i, i ^ partner) for i in range(count)])
            )

    widths = [level_shape(level, tokens)[1] for level in remote]
    local_outs = (
        [
            shape((2, HEAD, tokens), F32),
            shape((2, 2, tokens), F32),
            shape((2, HEAD, tokens // 2), F32),
            shape((2, 2, tokens // 2), F32),
            shape((2 * HEAD, 2 * LEAF), BF16),
            shape((2, 3 * LEAF, LANES), BF16),
        ]
        + [shape((2, 2 * HEAD, width), BF16) for width in widths]
        + [shape((2**i * width, LANES), F32) for i, width in enumerate(widths)]
        + [shape((16, 2**i * width), BF16) for i, width in enumerate(widths)]
    )
    local = pl.pallas_call(
        functools.partial(local_kernel, tokens, remote),
        out_shape=local_outs,
        in_specs=[HBM] + [VMEM] * 4,
        out_specs=[VMEM] * len(local_outs),
        scratch_shapes=[
            pltpu.SMEM(counts.shape, jnp.int32),
            pltpu.SemaphoreType.DMA(()),
            pltpu.VMEM((tokens, LANES), BF16),
        ],
        compiler_params=params(),
        cost_estimate=pl.CostEstimate(
            flops=2 * 128 * tokens * tokens + 2**31, bytes_accessed=8 * 2**20, transcendentals=2**22
        ),
        name="local_attention",
    )(counts, q.reshape(flat), order_here, kv_rows, v_cols)
    return pl.pallas_call(
        functools.partial(last_kernel, tokens, remote),
        out_shape=shape((2, HEAD, tokens), BF16),
        in_specs=[VMEM] * (len(local) + 4 + len(got)),
        out_specs=HBM,
        scratch_shapes=[
            pltpu.VMEM((2, HEAD, tokens), BF16),
            pltpu.SemaphoreType.DMA((leaves // 2,)),
        ],
        compiler_params=params(),
        cost_estimate=pl.CostEstimate(flops=2**30, bytes_accessed=4 * 2**20, transcendentals=2**20),
        name="remote_attention",
    )(*local[:6], kv_rows, v_cols, *local[6:], got_pair, got_step, *got)


def shards(q, k, v, order, counts):
    heads = q.shape[0]
    if heads % 2:
        q, k, v = (jnp.concatenate([x, jnp.zeros_like(x[:1])], axis=0) for x in (q, k, v))
    out = [
        head_pair(q[h : h + 2], k[h : h + 2], v[h : h + 2], order, counts)
        for h in range(0, q.shape[0], 2)
    ]
    out = out[0] if len(out) == 1 else jnp.concatenate(out, axis=0)
    return out[:heads] if heads % 2 else out


def solution(mesh):
    placed = (
        P("head", None, ("grp", "seq")),
        P("head", None, ("grp", "seq")),
        P("head", None, ("grp", "seq")),
        P(("grp", "seq"), None),
        P("grp"),
    )
    return jax.shard_map(
        shards,
        mesh=mesh,
        in_specs=placed,
        out_specs=P("head", None, ("grp", "seq")),
        check_vma=False,
    )
```

profile of v0, /device:TPU:0, one launch (start us, length us, event | category | flops | bytes accessed | tf_op | source)
XLA Modules:
  0.0 27.5 jit_solution(13131575134079193043)
XLA Ops:
  0.0 0.0 copy-start
  0.0 4.4 %gather_keys.1 = (bf16[2048,256]{1,0:T(8,128)(2,1)S(1)}, bf16[128,2048]{1,0:T(8,128)(2,1)S(1)}, s32[1,2048]{1,0:T(1,128)S(1)}, bf16[1536,128]{1,0:T(8,128)(2,1)S...) custom-call(s32[32]{0:T(128)} %counts_in.3, s32[1,2048]{1,0:T(1,128)} %order_in.1, ...), custom_call_target="tpu_custom_call" | custom-call | flops 2147483648 | bytes 4194304 | tf_op jit(solution)/shard_map/gather_keys/pallas_call | solution.py:536
  4.4 3.1 %collective-permute-start = (bf16[1536,128]{1,0:T(8,128)(2,1)S(1)}, bf16[1536,128]{1,0:T(8,128)(2,1)S(1)}, u32[]{:S(2)}, u32[]{:S(2)}) collective-permute-start(bf16[1536,128]{1,0:T(8,128)(2,1)S(1)} %get-tuple-element.38), channel_id=1, source_target_pairs={{0,4},{4,0},{8,12},{12,8},{1,5},{5,1},{9,13},{13,9},{2,6},{6,2},{1... | collective-permute-start | bytes 1179656 | tf_op jit(solution)/shard_map/ppermute | solution.py:556
  7.5 2.5 %collective-permute-start.3 = (bf16[512,128]{1,0:T(8,128)(2,1)S(1)}, bf16[512,128]{1,0:T(8,128)(2,1)S(1)}, u32[]{:S(2)}, u32[]{:S(2)}) collective-permute-start(bf16[512,128]{1,0:T(8,128)(2,1)S(1)} %get-tuple-element.40), channel_id=1, source_target_pairs={{0,12},{4,8},{8,4},{12,0},{1,13},{5,9},{9,5},{13,1},{2,14},{6,10},... | collective-permute-start | bytes 393224 | tf_op jit(solution)/shard_map/ppermute | solution.py:565
  9.9 0.1 collective-permute-start.2
  10.0 0.8 %collective-permute-start.1 = (bf16[512,128]{1,0:T(8,128)(2,1)S(1)}, bf16[512,128]{1,0:T(8,128)(2,1)S(1)}, u32[]{:S(2)}, u32[]{:S(2)}) collective-permute-start(bf16[512,128]{1,0:T(8,128)(2,1)S(1)} %get-tuple-element.39), channel_id=1, source_target_pairs={{4,8},{8,4},{5,9},{9,5},{6,10},{10,6},{7,11},{11,7},{20,24},{24,20... | collective-permute-start | bytes 393224 | tf_op jit(solution)/shard_map/ppermute | solution.py:560
  10.9 0.0 copy-start.1
  10.9 0.0 copy-done
  10.9 0.6 %copy-done.1 = s32[32]{0:T(128)S(1)} copy-done((s32[32]{0:T(128)S(1)}, s32[32]{0:T(128)}, u32[]{:S(2)}) %copy-start.1) | copy-done | bytes 152
  11.5 9.6 %local_attention.1 = (f32[2,64,2048]{2,1,0:T(8,128)S(1)}, f32[2,2,2048]{2,1,0:T(2,128)S(1)}, f32[2,64,1024]{2,1,0:T(8,128)S(1)}, f32[2,2,1024]{2,1,0:T(2,128)S(1...) custom-call(s32[32]{0:T(128)S(1)} %copy-done.1, ...), custom_call_target="tpu_custom_call" | custom-call | flops 3221225472 | bytes 8388608 | tf_op jit(solution)/shard_map/local_attention/pallas_call | solution.py:582
  21.1 0.0 collective-permute-done.1.rest_7_
  21.2 1.7 %collective-permute-done.3.rest_9_ = bf16[512,128]{1,0:T(8,128)(2,1)S(1)} collective-permute-done((bf16[512,128]{1,0:T(8,128)(2,1)S(1)}, bf16[512,128]{1,0:T(8,128)(2,1)S(1)}, u32[]{:S(2)}, u32[]{:S(2)}) %collective-permute-start.3) | collective-permute-done | bytes 131104 | tf_op jit(solution)/shard_map/ppermute | solution.py:565
  22.8 0.0 collective-permute-done.2.rest_8_
  22.8 0.0 collective-permute-done.rest_6_
  22.8 4.6 %remote_attention.1 = bf16[2,64,2048]{2,1,0:T(8,128)(2,1)} custom-call(f32[2,64,2048]{2,1,0:T(8,128)S(1)} %get-tuple-element.26.near_in, f32[2,2,2048]{2,1,0:T(2,128)S(1)} %get-tuple-element.27.near_stat, f32[2,64,1024]{2,1,0:T(8,128)S(1)} %get-tuple-element.28.far_in, f32[2,2,1024]{2,1,0:T(2,128)S(1)} %get-tuple-element.29.far_stat, ...), custom_call_target="tpu_custom_call" | custom-call | flops 1073741824 | bytes 4194304 | tf_op jit(solution)/shard_map/remote_attention/pallas_call | solution.py:598
Async XLA Ops:
  0.0 10.9 %copy-start = (bf16[2,64,2048]{2,1,0:T(8,128)(2,1)S(1)}, bf16[2,64,2048]{2,1,0:T(8,128)(2,1)}, u32[]{:S(2)}) copy-start(bf16[2,64,2048]{2,1,0:T(8,128)(2,1)} %param.5) | copy-start | bytes 1572868
  4.4 18.5 %collective-permute-start = (bf16[1536,128]{1,0:T(8,128)(2,1)S(1)}, bf16[1536,128]{1,0:T(8,128)(2,1)S(1)}, u32[]{:S(2)}, u32[]{:S(2)}) collective-permute-start(bf16[1536,128]{1,0:T(8,128)(2,1)S(1)} %get-tuple-element.38), channel_id=1, source_target_pairs={{0,4},{4,0},{8,12},{12,8},{1,5},{5,1},{9,13},{13,9},{2,6},{6,2},{1... | collective-permute-start | bytes 1179656 | tf_op jit(solution)/shard_map/ppermute | solution.py:556
  7.5 15.4 %collective-permute-start.3 = (bf16[512,128]{1,0:T(8,128)(2,1)S(1)}, bf16[512,128]{1,0:T(8,128)(2,1)S(1)}, u32[]{:S(2)}, u32[]{:S(2)}) collective-permute-start(bf16[512,128]{1,0:T(8,128)(2,1)S(1)} %get-tuple-element.40), channel_id=1, source_target_pairs={{0,12},{4,8},{8,4},{12,0},{1,13},{5,9},{9,5},{13,1},{2,14},{6,10},... | collective-permute-start | bytes 393224 | tf_op jit(solution)/shard_map/ppermute | solution.py:565
  9.9 12.9 %collective-permute-start.2 = (bf16[512,128]{1,0:T(8,128)(2,1)S(1)}, bf16[512,128]{1,0:T(8,128)(2,1)S(1)}, u32[]{:S(2)}, u32[]{:S(2)}) collective-permute-start(bf16[512,128]{1,0:T(8,128)(2,1)S(1)} %get-tuple-element.40), channel_id=1, source_target_pairs={{0,8},{4,12},{8,0},{12,4},{1,9},{5,13},{9,1},{13,5},{2,10},{6,14},... | collective-permute-start | bytes 393224 | tf_op jit(solution)/shard_map/ppermute | solution.py:565
  10.0 11.1 %collective-permute-start.1 = (bf16[512,128]{1,0:T(8,128)(2,1)S(1)}, bf16[512,128]{1,0:T(8,128)(2,1)S(1)}, u32[]{:S(2)}, u32[]{:S(2)}) collective-permute-start(bf16[512,128]{1,0:T(8,128)(2,1)S(1)} %get-tuple-element.39), channel_id=1, source_target_pairs={{4,8},{8,4},{5,9},{9,5},{6,10},{10,6},{7,11},{11,7},{20,24},{24,20... | collective-permute-start | bytes 393224 | tf_op jit(solution)/shard_map/ppermute | solution.py:560
  10.9 0.7 %copy-start.1 = (s32[32]{0:T(128)S(1)}, s32[32]{0:T(128)}, u32[]{:S(2)}) copy-start(s32[32]{0:T(128)} %counts_in.3) | copy-start | bytes 388
where the time goes:
time: 27.7 us; the launch traced here: 27.5 us
  Pallas kernels  18.5 us (67%)
  starting transfers between devices  6.52 us (24%)
  waiting for transfers between devices  1.66 us (6%)
  local copies, waits for them, and re-layouts  0.64 us (2%)
    pallas_call x1, Pallas kernels, head_pair(): pl.pallas_call(functools.partial(local_kernel, tokens, remote), out_shape...  9.59 us
    pallas_call x1, Pallas kernels, head_pair(): pl.pallas_call(functools.partial(last_kernel, tokens, remote), out_shape=...  4.56 us
    pallas_call x1, Pallas kernels, head_pair(): pl.pallas_call(functools.partial(kv_kernel, tokens, remote), out_shape=ou...  4.35 us
    ppermute x1, starting transfers between devices, head_pair(): got_pair = lax.ppermute(pair, 'seq', [(i, i ^ 1) for i in range(count)])  3.09 us
    ppermute x2, starting transfers between devices, head_pair(): lax.ppermute(packs[index - 1], 'seq', [(i, i ^ partner) for i in range(co...  2.59 us
    ppermute x2, waiting for transfers between devices, head_pair(): lax.ppermute(packs[index - 1], 'seq', [(i, i ^ partner) for i in range(co...  1.65 us
    ppermute x1, starting transfers between devices, head_pair(): lax.ppermute(step, 'seq', swaps)  0.84 us
    unnamed x4, local copies, waits for them, and re-layouts  0.64 us
  transfers between devices with their start and end apart: 4, of which 1 were waited for; matrix products, arithmetic and copies ran while one was open for 0% of the time, Pallas kernels for 35%

commit v1 on v0

v1 whole, which is shorter than its diff:
```python
import functools
import math

import jax
import jax.numpy as jnp
from jax import lax
from jax.experimental import pallas as pl
from jax.experimental.pallas import tpu as pltpu
from jax.sharding import PartitionSpec as P

LEAF = 256
HEAD = 64
LANES = 128
MASKED = -1e30
F32 = jnp.float32
BF16 = jnp.bfloat16
SCALE = math.log2(math.e) / math.sqrt(HEAD)
SENT = jnp.int16
CODE = 32000.0
PIECE = 4 * HEAD + 16


def dot(a, b):
    return lax.dot_general(a, b, (((1,), (0,)), ((), ())), preferred_element_type=F32)


def iota(shape, dim):
    return lax.broadcasted_iota(jnp.int32, shape, dim)


def bits(cond):
    return jnp.where(cond, 1.0, 0.0).astype(BF16)


def split(x, terms=2):
    out = []
    for _ in range(terms - 1):
        out.append(x.astype(BF16))
        x = x - out[-1].astype(F32)
    return out + [x.astype(BF16)]


def encode(keys, values):
    parts = []
    row = iota((16, keys.shape[1]), 0)
    exponents = jnp.zeros(row.shape, F32)
    for i, x in enumerate((keys, values)):
        largest = jnp.max(jnp.abs(x), axis=0, keepdims=True)
        exponent = jnp.floor(jnp.log2(jnp.maximum(largest, 2.0**-100))) + 1.0
        parts.append(jnp.round(x * (jnp.exp2(-exponent) * CODE)))
        exponents = jnp.where(row == i, exponent, exponents)
    codes = jnp.concatenate(parts + [exponents], axis=0).astype(jnp.int32).astype(SENT)
    return [codes[:, i : i + LANES] for i in range(0, codes.shape[1], LANES)]


def put(ref, at, pieces):
    for piece in pieces:
        ref[at : at + PIECE, :] = piece
        at += PIECE


def decode(ref, at, width):
    pieces = [ref[at + i * PIECE : at + (i + 1) * PIECE, :] for i in range(width // LANES)]
    x = jnp.concatenate(pieces, axis=1).astype(jnp.int32).astype(F32)
    scales = jnp.exp2(x[4 * HEAD :]) * (1.0 / CODE)
    return x[: 2 * HEAD] * scales[0:1], x[2 * HEAD : 4 * HEAD] * scales[1:2]


def one_hot(order_row, tokens):
    high = order_row // LEAF
    low = (order_row - high * LEAF).astype(F32).astype(BF16)
    slots = iota((LEAF, LEAF), 0).astype(F32).astype(BF16)
    base = jnp.where(slots == low, jnp.ones((), BF16), jnp.zeros((), BF16))
    return jnp.concatenate([base * bits(high == j) for j in range(tokens // LEAF)], axis=0)


def pool_rows(group, first_row, rows):
    return bits(iota((rows, LEAF), 1) // group + first_row == iota((rows, LEAF), 0))


def level_shape(level, tokens):
    group = 2**level
    rows = tokens // group
    return group, max(min(rows, LEAF), LANES), max(rows // LEAF, 1)


def place(level, leaf, tokens):
    group, rows, _ = level_shape(level, tokens)
    per_leaf = LEAF // group
    return (leaf * per_leaf) // rows, (leaf * per_leaf) % rows


def pooled(levels, leaf_values, tokens):
    sums = {}
    whole = [level for level in levels if LEAF // 2**level % 16 == 0]
    parts = [pool_rows(2**level, 0, LEAF // 2**level) for level in whole]
    for leaf, values in enumerate(leaf_values):
        both = dot(jnp.concatenate(parts, axis=0), values)
        at = 0
        for level in whole:
            count = LEAF // 2**level
            block, _ = place(level, leaf, tokens)
            sums.setdefault((level, block), []).append(both[at : at + count])
            at += count
    out = {at: jnp.concatenate(pieces, axis=0) for at, pieces in sums.items()}
    for level in levels:
        if level in whole:
            continue
        group, rows, _ = level_shape(level, tokens)
        for leaf, values in enumerate(leaf_values):
            block, first = place(level, leaf, tokens)
            piece = dot(pool_rows(group, first, rows), values)
            out[level, block] = out[level, block] + piece if leaf else piece
    return out


def mass(counts, first_leaf, leaves, group, rows):
    row = iota((16, rows), 1)
    per_leaf = LEAF // group
    leaf = row // per_leaf
    held = jnp.zeros(row.shape, jnp.int32)
    for n in range(leaves):
        held = jnp.where(leaf == n, counts[first_leaf + n], held)
    return jnp.clip(held - (row % per_leaf) * group, 0, group).astype(F32)


def valid_only(kv_rows, held):
    keep = bits(iota((LEAF, LANES), 0) < held)
    return kv_rows * jnp.concatenate([keep, keep], axis=1)


def near_marks(empty):
    return jnp.where((iota(empty.shape, 1) == 0) & empty, MASKED, 0.0).astype(BF16)


def far_keys(means, weight):
    hi, lo = split(means)
    mark = jnp.where((iota(weight.shape, 0) == 0) & (weight == 0.0), MASKED, 0.0).astype(BF16)
    rest = jnp.zeros((HEAD - 16, hi.shape[1]), BF16)
    out = []
    for h in range(2):
        here = slice(h * HEAD, (h + 1) * HEAD)
        out.append(
            jnp.concatenate([hi[here], lo[here], hi[here], mark, rest], axis=0).T
        )
    return out


def far_values(sums, mass_rows):
    hi, lo = split(sums)
    mass_rows = mass_rows.astype(BF16)
    return [
        jnp.concatenate([hi[h * HEAD : (h + 1) * HEAD], lo[h * HEAD : (h + 1) * HEAD], mass_rows], axis=0)
        for h in range(2)
    ]


def near_scores(k_window, mark, query):
    none = jnp.zeros((HEAD, LEAF), BF16)
    right = jnp.concatenate(
        [
            jnp.concatenate([query[:HEAD], none], axis=1),
            jnp.concatenate([none, query[HEAD:]], axis=1),
            bits(iota((LANES, 2 * LEAF), 0) == 0),
        ],
        axis=0,
    )
    left = jnp.concatenate([k_window, mark], axis=1)
    return [dot(left[i * LEAF : (i + 1) * LEAF], right) for i in range(3)]


def near(scores, v_window, h):
    scores = [piece[:, h * LEAF : (h + 1) * LEAF] for piece in scores]
    top = functools.reduce(jnp.maximum, [jnp.max(x, axis=0, keepdims=True) for x in scores])
    sums = totals = 0.0
    for i, piece in enumerate(scores):
        weights = jnp.exp2((piece - top) * SCALE)
        totals = totals + jnp.sum(weights, axis=0, keepdims=True)
        value = v_window[h * HEAD : (h + 1) * HEAD, i * LEAF : (i + 1) * LEAF]
        sums = sums + dot(value, weights.astype(BF16))
    return top * SCALE, sums, totals


def far_scores(keys, query):
    hi, lo = query[:HEAD], query[HEAD:]
    flag = bits(iota((HEAD, query.shape[1]), 0) == 0)
    return dot(keys, jnp.concatenate([hi, hi, lo, flag], axis=0))


def far(scores, value):
    top = jnp.max(scores, axis=0, keepdims=True).astype(BF16).astype(F32)
    w_hi, w_lo = split(jnp.exp2(scores - top))
    out = dot(jnp.concatenate([value, value], axis=1), jnp.concatenate([w_hi, w_lo], axis=0))
    return top, out[:HEAD] + out[HEAD : 2 * HEAD], out[2 * HEAD : 2 * HEAD + 1]


def staggered(units, ahead=1):
    held = []
    for first, second in units:
        held.append((second, first()))
        if len(held) > ahead:
            second, scores = held.pop(0)
            second(scores)
    for second, scores in held:
        second(scores)


def to_spread(term):
    top, sums, totals = term
    row = iota((16, sums.shape[1]), 0)
    t_hi, t_lo = split(totals)
    tail = jnp.where(row == 0, t_hi.astype(F32), jnp.where(row == 1, t_lo.astype(F32), top))
    hi, lo = split(sums)
    return jnp.concatenate([hi, lo, tail.astype(BF16)], axis=0)


def spread_matrix(times, first, width=LEAF):
    size = (LANES, width)
    return bits(iota(size, 0) == iota(size, 1) // times + first)


def spread(rows, matrix):
    x = dot(rows, matrix)
    tail = x[2 * HEAD :]
    return tail[2:3], x[:HEAD] + x[HEAD : 2 * HEAD], tail[0:1] + tail[1:2]


def merge(terms):
    top = functools.reduce(jnp.maximum, [t[0] for t in terms])
    sums = totals = 0.0
    for t in terms:
        factor = jnp.exp2(t[0] - top)
        sums = sums + t[1] * factor
        totals = totals + t[2] * factor
    return top, sums, totals


def halo_rows():
    return LEAF // LANES * PIECE


def joined(tokens, step):
    return step.shape[0] > halo_rows()


def pack_rows(index, tokens, level):
    rows = level_shape(level, tokens)[1] // LANES * PIECE
    return rows + (halo_rows() if index == 0 else 0)


def kv_kernel(
    tokens, remote, counts_in, order_in, k_in, v_in, q_in, kv_rows, v_cols, q_cols, pair, step, *rest
):
    packs, (counts, order, k, v, q, sems) = rest[: len(remote) - 1], rest[len(remote) - 1 :]
    copies = [
        pltpu.make_async_copy(source, target, sems.at[i])
        for i, (source, target) in enumerate(
            ((order_in, order), (k_in, k), (v_in, v), (q_in, q), (counts_in, counts))
        )
    ]
    for copy in copies:
        copy.start()
    for copy in copies:
        copy.wait()
    rank = lax.axis_index("seq")
    leaves = tokens // LEAF
    joint = jnp.concatenate([k[...], v[...], q[...]], axis=0)
    masked = []
    ends = {}
    for n in range(leaves):
        cols = slice(n * LEAF, (n + 1) * LEAF)
        got = dot(joint, one_hot(order[:, cols], tokens))
        got16 = got.astype(BF16)
        rows = got16[: 2 * LANES].T
        q_cols[:, cols] = got16[2 * LANES :]
        kv_rows[cols, :] = rows
        v_cols[:, cols] = got16[LANES : 2 * LANES]
        if n in (0, leaves - 1):
            ends[n] = got
        masked.append(valid_only(rows, counts[rank * leaves + n]))
    odd = rank % 2 == 1

    @pl.when(odd)
    def _():
        put(pair, 0, encode(ends[0][:LANES], ends[0][LANES : 2 * LANES]))
        put(step, 0, encode(ends[leaves - 1][:LANES], ends[leaves - 1][LANES : 2 * LANES]))

    @pl.when(jnp.logical_not(odd))
    def _():
        put(pair, 0, encode(ends[leaves - 1][:LANES], ends[leaves - 1][LANES : 2 * LANES]))
        put(step, 0, encode(ends[0][:LANES], ends[0][LANES : 2 * LANES]))

    sums = pooled(remote, masked, tokens)
    for index, level in enumerate(remote):
        codes = coarse_codes(counts, rank, level, sums[level, 0], tokens)
        if index == 0:
            put(pair, halo_rows(), codes)
        else:
            put(packs[index - 1], 0, codes)
        if index == 1 and joined(tokens, step):
            put(step, halo_rows(), codes)


def coarse_codes(counts, rank, level, sums, tokens):
    group, rows, _ = level_shape(level, tokens)
    leaves = tokens // LEAF
    weight = mass(counts, rank * leaves, leaves, group, rows)[:1]
    sums = sums.T
    return encode(sums[:LANES] / jnp.maximum(weight, 1.0), sums[LANES:])


def local_kernel(tokens, remote, counts_in, q_cols, kv_rows, v_cols, *rest):
    levels = len(remote)
    sums_out, stat_out, end_marks, matrices = rest[:4]
    queries_out, mass_out = rest[4 : 4 + levels], rest[4 + levels : 4 + 2 * levels]
    counts, sem, mark = rest[4 + 2 * levels :]
    copy = pltpu.make_async_copy(counts_in, counts, sem)
    copy.start()
    rank = lax.axis_index("seq")
    count = lax.axis_size("seq")
    leaves = tokens // LEAF
    first_leaf = rank * leaves
    copy.wait()
    near_terms = {}
    for n in range(leaves):
        rows = slice(n * LEAF, (n + 1) * LEAF)
        mark[rows, :] = near_marks(iota((LEAF, LANES), 0) >= counts[first_leaf + n])

    def near_unit(n):
        cols = slice(n * LEAF, (n + 1) * LEAF)
        window = slice((n - 1) * LEAF, (n + 2) * LEAF)

        def first():
            return near_scores(kv_rows[window, :LANES], mark[window, :], q_cols[:, cols])

        def second(scores):
            for h in range(2):
                near_terms[n, h] = near(scores, v_cols[:, window], h)

        return first, second

    staggered([near_unit(n) for n in range(1, leaves - 1)])
    leaf_q = [q_cols[:, n * LEAF : (n + 1) * LEAF].T for n in range(leaves)]
    q_sums = pooled((1, 2) + tuple(remote), leaf_q, tokens)

    def queries(level, block):
        hi, lo = split(q_sums[level, block].T * (SCALE / 2**level))
        return [
            jnp.concatenate([x[h * HEAD : (h + 1) * HEAD] for x in (hi, lo)], axis=0)
            for h in range(2)
        ]

    masked = [
        valid_only(kv_rows[n * LEAF : (n + 1) * LEAF, :], counts[first_leaf + n])
        for n in range(leaves)
    ]
    kv_sums = pooled((1, 2), masked, tokens)
    results = {}
    units = []
    for level in (2, 1):
        group, rows, blocks = level_shape(level, tokens)
        per_block = rows * group // LEAF
        for block in range(blocks):
            weight = mass(counts, first_leaf + block * per_block, per_block, group, rows)
            sums = kv_sums[level, block].T
            keys = far_keys(sums[:LANES] / jnp.maximum(weight[:1], 1.0), weight)
            values = far_values(sums[LANES:], weight)
            query = queries(level, block ^ 1)
            for h in range(2):

                def second(scores, at=(level, block ^ 1, h), value=values[h]):
                    results[at] = far(scores, value)

                units.append((functools.partial(far_scores, keys[h], query[h]), second))
    staggered(units, 4)
    for index, level in enumerate(remote):
        block = queries(level, 0)
        for h in range(2):
            queries_out[index][h] = block[h]
    twice = spread_matrix(2, 0)
    matrices[0] = twice
    for j in range(4):
        matrices[j + 1] = spread_matrix(8, j * 32)
    for block in range(leaves // 2):
        for h in range(2):
            coarse = to_spread(results[2, block // 2, h])
            half = slice((block % 2) * LANES, (block % 2 + 1) * LANES)
            fine = to_spread(merge([results[1, block, h], spread(coarse[:, half], twice)]))
            for part in range(2):
                n = 2 * block + part
                cols = slice(n * LEAF, (n + 1) * LEAF)
                term = spread(fine[:, part * LANES : (part + 1) * LANES], twice)
                if 0 < n < leaves - 1:
                    term = merge([near_terms[n, h], term])
                stat_out[h, 0:1, cols], sums_out[h, :, cols], stat_out[h, 1:2, cols] = term

    row = iota((LEAF, LANES), 0)
    for side, leaf in ((0, first_leaf - 1), (1, first_leaf + leaves)):
        there = jnp.logical_and(leaf >= 0, leaf < count * leaves)
        held = jnp.where(there, counts[jnp.clip(leaf, 0, count * leaves - 1)], 0)
        end_marks[side, :LEAF] = near_marks(row >= held)
        for i in range(2):
            inner = first_leaf + side * (leaves - 2) + i
            end_marks[side, (i + 1) * LEAF : (i + 2) * LEAF] = near_marks(row >= counts[inner])
    for index, level in enumerate(remote):
        group, rows, _ = level_shape(level, tokens)
        for i in range(2**index):
            start = (rank ^ (2**index + i)) * leaves
            mass_out[index][:, i * rows : (i + 1) * rows] = mass(counts, start, leaves, group, rows)


def last_kernel(
    tokens, remote, q_cols, kv_rows, v_cols, sums_in, stat_in, end_marks, matrices, *rest
):
    levels = len(remote)
    queries, mass_in = rest[:levels], rest[levels : 2 * levels]
    pair, step = rest[2 * levels : 2 * levels + 2]
    packs = rest[2 * levels + 2 : -3]
    out, stage, sems = rest[-3:]
    rank = lax.axis_index("seq")
    leaves = tokens // LEAF
    flag = jnp.where(rank % 2 == 1, 1, 0)
    ends = {}
    results = {}

    halo_pair = decode(pair, 0, LEAF)
    halo_step = decode(step, 0, LEAF)

    def near_unit(side):
        own = flag if side == 0 else 1 - flag
        inner = slice(side * (leaves - 2) * LEAF, (side * (leaves - 2) + 2) * LEAF)
        keys, values = [
            jnp.where(own == 1, here, there).astype(BF16)
            for here, there in zip(halo_pair, halo_step)
        ]

        def first():
            return near_scores(
                jnp.concatenate([keys.T, kv_rows[inner, :LANES]], axis=0),
                end_marks[side],
                q_cols[:, side * (leaves - 1) * LEAF : (side * (leaves - 1) + 1) * LEAF],
            )

        def second(scores):
            window = jnp.concatenate([values, v_cols[:, inner]], axis=1)
            for h in range(2):
                ends[side * (leaves - 1), h] = near(scores, window, h)

        return first, second

    def far_units(index):
        level = remote[index]
        group, rows, _ = level_shape(level, tokens)
        if index == 0:
            fields = [decode(pair, halo_rows(), rows)]
        else:
            refs = [(packs[2**index - 2 + i], 0) for i in range(2**index - (index == 1 and joined(tokens, step)))]
            if index == 1 and joined(tokens, step):
                refs.append((step, halo_rows()))
            fields = [decode(ref, at, rows) for ref, at in refs]
        means, sums = [jnp.concatenate(field, axis=1) for field in zip(*fields)]
        keys = far_keys(means, mass_in[index][...])
        values = far_values(sums, mass_in[index][...])
        units = []
        for h in range(2):

            def second(scores, h=h):
                results[index, h] = far(scores, values[h])

            units.append((functools.partial(far_scores, keys[h], queries[index][h]), second))
        return units

    units = [near_unit(0), near_unit(1)]
    for index in range(levels):
        units += far_units(index)
    staggered(units, 2)

    coarse = []
    for h in range(2):
        merged = results[levels - 1, h]
        for index in reversed(range(levels - 1)):
            rows = level_shape(remote[index], tokens)[1]
            merged = merge(
                [results[index, h], spread(to_spread(merged)[:, :LANES], matrices[0, :, :rows])]
            )
        coarse.append(to_spread(merged))
    copies = []
    for n in range(leaves):
        cols = slice(n * LEAF, (n + 1) * LEAF)
        half = slice(n // 4 * LANES, (n // 4 + 1) * LANES)
        for h in range(2):
            terms = [
                (stat_in[h, 0:1, cols], sums_in[h, :, cols], stat_in[h, 1:2, cols]),
                spread(coarse[h][:, half], matrices[n % 4 + 1]),
            ]
            if (n, h) in ends:
                terms.append(ends[n, h])
            _, sums, totals = merge(terms)
            stage[h, :, cols] = (sums * (1.0 / totals)).astype(BF16)
        if n % 2:
            both = slice((n - 1) * LEAF, (n + 1) * LEAF)
            copies.append(
                pltpu.make_async_copy(stage.at[:, :, both], out.at[:, :, both], sems.at[n // 2])
            )
            copies[-1].start()
    for copy in copies:
        copy.wait()


VMEM = pl.BlockSpec(memory_space=pltpu.VMEM)
ANY = pl.BlockSpec(memory_space=pl.ANY)


def params():
    return pltpu.CompilerParams(vmem_limit_bytes=48 * 2**20)


def head_pair(q, k, v, order, counts):
    tokens = q.shape[2]
    leaves = tokens // LEAF
    count = lax.axis_size("seq")
    depth = (tokens * count // LEAF).bit_length() - 1
    remote = tuple(range(leaves.bit_length() - 1, depth))
    four = False
    flat = (2 * HEAD, tokens)
    shape = jax.ShapeDtypeStruct
    outs = [
        shape((tokens, 4 * HEAD), BF16),
        shape(flat, BF16),
        shape(flat, BF16),
        shape((pack_rows(0, tokens, remote[0]), LANES), SENT),
        shape((halo_rows() + (pack_rows(1, tokens, remote[1]) if four else 0), LANES), SENT),
    ] + [shape((pack_rows(i, tokens, remote[i]), LANES), SENT) for i in range(1, len(remote))]
    counts, order, k, v, q = (
        pltpu.with_memory_space_constraint(x, pltpu.HBM)
        for x in (counts, order, k.reshape(flat), v.reshape(flat), q.reshape(flat))
    )
    kv_rows, v_cols, q_cols, pair, step, *packs = pl.pallas_call(
        functools.partial(kv_kernel, tokens, remote),
        out_shape=outs,
        in_specs=[ANY] * 5,
        out_specs=[VMEM] * len(outs),
        scratch_shapes=[
            pltpu.SMEM(counts.shape, jnp.int32),
            pltpu.VMEM((1, tokens), jnp.int32),
            pltpu.VMEM(flat, BF16),
            pltpu.VMEM(flat, BF16),
            pltpu.VMEM(flat, BF16),
            pltpu.SemaphoreType.DMA((5,)),
        ],
        compiler_params=params(),
        cost_estimate=pl.CostEstimate(
            flops=2 * 256 * tokens * tokens, bytes_accessed=4 * 2**20, transcendentals=0
        ),
        name="gather_keys",
    )(counts, order, k, v, q)

    got_pair = lax.ppermute(pair, "seq", [(i, i ^ 1) for i in range(count)])
    got = []
    for index in range(1, len(remote)):
        for partner in range(2**index, 2 ** (index + 1)):
            if four and partner == 3:
                continue
            got.append(
                lax.ppermute(packs[index - 1], "seq", [(i, i ^ partner) for i in range(count)])
            )
    swaps = [(i, count - 1 - i) for i in range(count)] if four else []
    for i in range(1, count - 1, 2):
        swaps += [] if four else [(i, i + 1), (i + 1, i)]
    got_step = lax.ppermute(step, "seq", swaps) if swaps else jnp.zeros_like(step)

    widths = [level_shape(level, tokens)[1] for level in remote]
    outs = (
        [shape((2, HEAD, tokens), F32), shape((2, 2, tokens), F32)]
        + [shape((2, 3 * LEAF, LANES), BF16), shape((5, LANES, LEAF), BF16)]
        + [shape((2, 2 * HEAD, width), BF16) for width in widths]
        + [shape((16, 2**i * width), F32) for i, width in enumerate(widths)]
    )
    local = pl.pallas_call(
        functools.partial(local_kernel, tokens, remote),
        out_shape=outs,
        in_specs=[ANY] + [VMEM] * 3,
        out_specs=[VMEM] * len(outs),
        scratch_shapes=[
            pltpu.SMEM(counts.shape, jnp.int32),
            pltpu.SemaphoreType.DMA(()),
            pltpu.VMEM((tokens, LANES), BF16),
        ],
        compiler_params=params(),
        cost_estimate=pl.CostEstimate(flops=2**33, bytes_accessed=8 * 2**20, transcendentals=2**22),
        name="local_attention",
    )(counts, q_cols, kv_rows, v_cols)
    return pl.pallas_call(
        functools.partial(last_kernel, tokens, remote),
        out_shape=shape((2, HEAD, tokens), BF16),
        in_specs=[VMEM] * (5 + len(local) + len(got)),
        out_specs=ANY,
        scratch_shapes=[
            pltpu.VMEM((2, HEAD, tokens), BF16),
            pltpu.SemaphoreType.DMA((leaves // 2,)),
        ],
        compiler_params=params(),
        cost_estimate=pl.CostEstimate(flops=2**30, bytes_accessed=4 * 2**20, transcendentals=2**20),
        name="remote_attention",
    )(q_cols, kv_rows, v_cols, *local, got_pair, got_step, *got)


def shards(q, k, v, order, counts):
    heads = q.shape[0]
    if heads % 2:
        q, k, v = (jnp.concatenate([x, jnp.zeros_like(x[:1])], axis=0) for x in (q, k, v))
    out = [
        head_pair(q[h : h + 2], k[h : h + 2], v[h : h + 2], order, counts)
        for h in range(0, q.shape[0], 2)
    ]
    out = out[0] if len(out) == 1 else jnp.concatenate(out, axis=0)
    return out[:heads] if heads % 2 else out


def solution(mesh):
    placed = (
        P("head", None, ("grp", "seq")),
        P("head", None, ("grp", "seq")),
        P("head", None, ("grp", "seq")),
        P(("grp", "seq"), None),
        P("grp"),
    )
    return jax.shard_map(
        shards,
        mesh=mesh,
        in_specs=placed,
        out_specs=P("head", None, ("grp", "seq")),
        check_vma=False,
    )
```

time: 27.7 us -> 26.9 us (0.971)
  starting transfers between devices: 6.52 us -> 10.6 us
  Pallas kernels: 18.5 us -> 16 us
  waiting for transfers between devices: 1.66 us -> 0.01 us
  local copies, waits for them, and re-layouts: 0.64 us -> 0 us
    ppermute x2, starting transfers between devices: 2.59 us -> 5.11 us  [head_pair(): lax.ppermute(packs[index - 1], 'seq', [(i, i ^ partner) for i in range(co...]
    pallas_call x1, Pallas kernels: 9.59 us -> 7.52 us  [head_pair(): pl.pallas_call(functools.partial(local_kernel, tokens, remote), out_shape...]
    ppermute x1, starting transfers between devices: 3.09 us -> 4.79 us  [head_pair(): got_pair = lax.ppermute(pair, 'seq', [(i, i ^ 1) for i in range(count)])]
    ppermute x2, waiting for transfers between devices: 1.65 us -> 0.01 us  [head_pair(): lax.ppermute(packs[index - 1], 'seq', [(i, i ^ partner) for i in range(co...]
    pallas_call x1, Pallas kernels: 4.56 us -> 3.06 us  [head_pair(): pl.pallas_call(functools.partial(last_kernel, tokens, remote), out_shape=...]
    pallas_call x1, Pallas kernels: 4.35 us -> 5.45 us  [head_pair(): pl.pallas_call(functools.partial(kv_kernel, tokens, remote), out_shape=ou...]
    unnamed x4 -> x0, local copies, waits for them, and re-layouts: 0.64 us -> none
  transfers between devices with their start and end apart: 4 -> 4, of which waited for: 1 -> 0; matrix products, arithmetic and copies ran while one was open for 0% -> 0% of each run, Pallas kernels for 35% -> 28%
where the time goes in v1:
time: 26.9 us; the launch traced here: 26.7 us
  Pallas kernels  16 us (59%)
  starting transfers between devices  10.6 us (39%)
    pallas_call x1, Pallas kernels, head_pair(): pl.pallas_call(functools.partial(local_kernel, tokens, remote), out_shape...  7.52 us
    pallas_call x1, Pallas kernels, head_pair(): pl.pallas_call(functools.partial(kv_kernel, tokens, remote), out_shape=ou...  5.45 us
    ppermute x2, starting transfers between devices, head_pair(): lax.ppermute(packs[index - 1], 'seq', [(i, i ^ partner) for i in range(co...  5.11 us
    ppermute x1, starting transfers between devices, head_pair(): got_pair = lax.ppermute(pair, 'seq', [(i, i ^ 1) for i in range(count)])  4.79 us
    pallas_call x1, Pallas kernels, head_pair(): pl.pallas_call(functools.partial(last_kernel, tokens, remote), out_shape=...  3.06 us
    ppermute x1, starting transfers between devices, head_pair(): lax.ppermute(step, 'seq', swaps)  0.66 us
  transfers between devices with their start and end apart: 4, of which 0 were waited for; matrix products, arithmetic and copies ran while one was open for 0% of the time, Pallas kernels for 28%

profile of v1, /device:TPU:0, one launch (start us, length us, event | category | flops | bytes accessed | tf_op | source)
XLA Modules:
  0.0 26.7 jit_solution(9339438847583900256)
XLA Ops:
  0.0 5.5 %gather_keys.1 = (bf16[2048,256]{1,0:T(8,128)(2,1)S(1)}, bf16[128,2048]{1,0:T(8,128)(2,1)S(1)}, bf16[128,2048]{1,0:T(8,128)(2,1)S(1)}, s16[1088,128]{1,0:T(8,128...) custom-call(s32[32]{0:T(128)} %counts_in.3, s32[1,2048]{1,0:T(1,128)} %order_in.1, ...), custom_call_target="tpu_custom_call" | custom-call | flops 2147483648 | bytes 4194304 | tf_op jit(solution)/shard_map/gather_keys/pallas_call | solution.py:538
  5.5 5.1 %collective-permute-start.3 = (s16[272,128]{1,0:T(8,128)(2,1)S(1)}, s16[272,128]{1,0:T(8,128)(2,1)S(1)}, u32[]{:S(2)}, u32[]{:S(2)}) collective-permute-start(s16[272,128]{1,0:T(8,128)(2,1)S(1)} %get-tuple-element.32), channel_id=1, source_target_pairs={{0,12},{4,8},{8,4},{12,0},{1,13},{5,9},{9,5},{13,1},{2,14},{6,10},... | collective-permute-start | bytes 208904 | tf_op jit(solution)/shard_map/ppermute | solution.py:565
  10.6 0.0 collective-permute-start.2
  10.6 0.7 %collective-permute-start.1 = (s16[544,128]{1,0:T(8,128)(2,1)S(1)}, s16[544,128]{1,0:T(8,128)(2,1)S(1)}, u32[]{:S(2)}, u32[]{:S(2)}) collective-permute-start(s16[544,128]{1,0:T(8,128)(2,1)S(1)} %get-tuple-element.31), channel_id=1, source_target_pairs={{4,8},{8,4},{5,9},{9,5},{6,10},{10,6},{7,11},{11,7},{20,24},{24,20... | collective-permute-start | bytes 417800 | tf_op jit(solution)/shard_map/ppermute | solution.py:570
  11.2 4.8 %collective-permute-start = (s16[1088,128]{1,0:T(8,128)(2,1)S(1)}, s16[1088,128]{1,0:T(8,128)(2,1)S(1)}, u32[]{:S(2)}, u32[]{:S(2)}) collective-permute-start(s16[1088,128]{1,0:T(8,128)(2,1)S(1)} %get-tuple-element.30), channel_id=1, source_target_pairs={{0,4},{4,0},{8,12},{12,8},{1,5},{5,1},{9,13},{13,9},{2,6},{6,2},{1... | collective-permute-start | bytes 835592 | tf_op jit(solution)/shard_map/ppermute | solution.py:558
  16.0 7.5 %local_attention.1 = (f32[2,64,2048]{2,1,0:T(8,128)S(1)}, f32[2,2,2048]{2,1,0:T(2,128)S(1)}, bf16[2,768,128]{2,1,0:T(8,128)(2,1)S(1)}, bf16[5,128,256]{2,1,0:T(8...) custom-call(s32[32]{0:T(128)} %counts_in.3, ...), custom_call_target="tpu_custom_call" | custom-call | flops 8589934592 | bytes 8388608 | tf_op jit(solution)/shard_map/local_attention/pallas_call | solution.py:579
  23.6 0.0 collective-permute-done.3.rest_7_
  23.6 0.0 collective-permute-done.2.rest_6_
  23.6 0.0 collective-permute-done.1.rest_5_
  23.6 0.0 collective-permute-done.rest_4_
  23.6 3.1 %remote_attention.1 = bf16[2,64,2048]{2,1,0:T(8,128)(2,1)} custom-call(bf16[128,2048]{1,0:T(8,128)(2,1)S(1)} %get-tuple-element.19.q_cols, bf16[2048,256]{1,0:T(8,128)(2,1)S(1)} %get-tuple-element.20.kv_rows, bf16[128,2048]{1,0:T(8,128)(2,1)S(1)} %get-tuple-element.21.v_cols, f32[2,64,2048]{2,1,0:T(8,128)S(1)} %get-tuple-element.22.sums_in, ...), custom_call_target="tpu_custom_call" | custom-call | flops 1073741824 | bytes 4194304 | tf_op jit(solution)/shard_map/remote_attention/pallas_call | solution.py:593
Async XLA Ops:
  5.5 18.1 %collective-permute-start.3 = (s16[272,128]{1,0:T(8,128)(2,1)S(1)}, s16[272,128]{1,0:T(8,128)(2,1)S(1)}, u32[]{:S(2)}, u32[]{:S(2)}) collective-permute-start(s16[272,128]{1,0:T(8,128)(2,1)S(1)} %get-tuple-element.32), channel_id=1, source_target_pairs={{0,12},{4,8},{8,4},{12,0},{1,13},{5,9},{9,5},{13,1},{2,14},{6,10},... | collective-permute-start | bytes 208904 | tf_op jit(solution)/shard_map/ppermute | solution.py:565
  10.6 13.0 %collective-permute-start.2 = (s16[272,128]{1,0:T(8,128)(2,1)S(1)}, s16[272,128]{1,0:T(8,128)(2,1)S(1)}, u32[]{:S(2)}, u32[]{:S(2)}) collective-permute-start(s16[272,128]{1,0:T(8,128)(2,1)S(1)} %get-tuple-element.32), channel_id=1, source_target_pairs={{0,8},{4,12},{8,0},{12,4},{1,9},{5,13},{9,1},{13,5},{2,10},{6,14},... | collective-permute-start | bytes 208904 | tf_op jit(solution)/shard_map/ppermute | solution.py:565
  10.6 13.0 %collective-permute-start.1 = (s16[544,128]{1,0:T(8,128)(2,1)S(1)}, s16[544,128]{1,0:T(8,128)(2,1)S(1)}, u32[]{:S(2)}, u32[]{:S(2)}) collective-permute-start(s16[544,128]{1,0:T(8,128)(2,1)S(1)} %get-tuple-element.31), channel_id=1, source_target_pairs={{4,8},{8,4},{5,9},{9,5},{6,10},{10,6},{7,11},{11,7},{20,24},{24,20... | collective-permute-start | bytes 417800 | tf_op jit(solution)/shard_map/ppermute | solution.py:570
  11.2 12.3 %collective-permute-start = (s16[1088,128]{1,0:T(8,128)(2,1)S(1)}, s16[1088,128]{1,0:T(8,128)(2,1)S(1)}, u32[]{:S(2)}, u32[]{:S(2)}) collective-permute-start(s16[1088,128]{1,0:T(8,128)(2,1)S(1)} %get-tuple-element.30), channel_id=1, source_target_pairs={{0,4},{4,0},{8,12},{12,8},{1,5},{5,1},{9,13},{13,9},{2,6},{6,2},{1... | collective-permute-start | bytes 835592 | tf_op jit(solution)/shard_map/ppermute | solution.py:558

commit v2 on v1

--- a/solution.py
+++ b/solution.py
@@ -219,8 +219,7 @@
     return bits(iota(size, 0) == iota(size, 1) // times + first)
 
 
-def spread(rows, matrix):
-    x = dot(rows, matrix)
+def from_spread(x):
     tail = x[2 * HEAD :]
     return tail[2:3], x[:HEAD] + x[HEAD : 2 * HEAD], tail[0:1] + tail[1:2]
 
@@ -239,66 +238,62 @@
     return LEAF // LANES * PIECE
 
 
-def joined(tokens, step):
-    return step.shape[0] > halo_rows()
-
-
 def pack_rows(index, tokens, level):
     rows = level_shape(level, tokens)[1] // LANES * PIECE
     return rows + (halo_rows() if index == 0 else 0)
 
 
-def kv_kernel(
-    tokens, remote, counts_in, order_in, k_in, v_in, q_in, kv_rows, v_cols, q_cols, pair, step, *rest
+def key_kernel(
+    tokens, remote, counts_in, order_in, k_in, v_in, kv_rows, v_cols, order, other, pair, *rest
 ):
-    packs, (counts, order, k, v, q, sems) = rest[: len(remote) - 1], rest[len(remote) - 1 :]
+    sums_out, (counts, k, v, sems) = rest[: len(remote) - 1], rest[len(remote) - 1 :]
     copies = [
         pltpu.make_async_copy(source, target, sems.at[i])
         for i, (source, target) in enumerate(
-            ((order_in, order), (k_in, k), (v_in, v), (q_in, q), (counts_in, counts))
+            ((order_in, order), (k_in, k), (v_in, v), (counts_in, counts))
         )
     ]
     for copy in copies:
         copy.start()
-    for copy in copies:
-        copy.wait()
     rank = lax.axis_index("seq")
     leaves = tokens // LEAF
-    joint = jnp.concatenate([k[...], v[...], q[...]], axis=0)
+    copies[0].wait()
+    first = one_hot(order[:, :LEAF], tokens)
+    for copy in copies[1:]:
+        copy.wait()
+    joint = jnp.concatenate([k[...], v[...]], axis=0)
     masked = []
-    ends = {}
+    got = []
     for n in range(leaves):
         cols = slice(n * LEAF, (n + 1) * LEAF)
-        got = dot(joint, one_hot(order[:, cols], tokens))
-        got16 = got.astype(BF16)
-        rows = got16[: 2 * LANES].T
-        q_cols[:, cols] = got16[2 * LANES :]
+        got.append(dot(joint, one_hot(order[:, cols], tokens) if n else first).astype(BF16))
+        rows = got[n].T
         kv_rows[cols, :] = rows
-        v_cols[:, cols] = got16[LANES : 2 * LANES]
-        if n in (0, leaves - 1):
-            ends[n] = got
+        v_cols[:, cols] = got[n][LANES:]
         masked.append(valid_only(rows, counts[rank * leaves + n]))
-    odd = rank % 2 == 1
-
-    @pl.when(odd)
-    def _():
-        put(pair, 0, encode(ends[0][:LANES], ends[0][LANES : 2 * LANES]))
-        put(step, 0, encode(ends[leaves - 1][:LANES], ends[leaves - 1][LANES : 2 * LANES]))
-
-    @pl.when(jnp.logical_not(odd))
-    def _():
-        put(pair, 0, encode(ends[leaves - 1][:LANES], ends[leaves - 1][LANES : 2 * LANES]))
-        put(step, 0, encode(ends[0][:LANES], ends[0][LANES : 2 * LANES]))
-
+    odd = jnp.where(rank % 2 == 1, 1, 0)
+    low, high = got[0].astype(F32), got[-1].astype(F32)
+    halo = jnp.where(odd == 1, low, high)
+    put(pair, 0, encode(halo[:LANES], halo[LANES:]))
+    other[...] = jnp.where(odd == 1, high, low).astype(BF16)
     sums = pooled(remote, masked, tokens)
-    for index, level in enumerate(remote):
-        codes = coarse_codes(counts, rank, level, sums[level, 0], tokens)
-        if index == 0:
-            put(pair, halo_rows(), codes)
-        else:
-            put(packs[index - 1], 0, codes)
-        if index == 1 and joined(tokens, step):
-            put(step, halo_rows(), codes)
+    put(pair, halo_rows(), coarse_codes(counts, rank, remote[0], sums[remote[0], 0], tokens))
+    for ref, level in zip(sums_out, remote[1:]):
+        ref[...] = sums[level, 0]
+
+
+def pack_kernel(tokens, remote, counts_in, other, *rest):
+    levels = len(remote) - 1
+    sums, step, packs = rest[:levels], rest[levels], rest[levels + 1 : 2 * levels + 1]
+    counts, sem = rest[2 * levels + 1 :]
+    copy = pltpu.make_async_copy(counts_in, counts, sem)
+    copy.start()
+    rank = lax.axis_index("seq")
+    halo = other[...].astype(F32)
+    put(step, 0, encode(halo[:LANES], halo[LANES:]))
+    copy.wait()
+    for i, level in enumerate(remote[1:]):
+        put(packs[i], 0, coarse_codes(counts, rank, level, sums[i][...], tokens))
 
 
 def coarse_codes(counts, rank, level, sums, tokens):
@@ -309,7 +304,7 @@
     return encode(sums[:LANES] / jnp.maximum(weight, 1.0), sums[LANES:])
 
 
-def local_kernel(tokens, remote, counts_in, q_cols, kv_rows, v_cols, *rest):
+def local_kernel(tokens, remote, counts_in, q, order, kv_rows, v_cols, q_cols, *rest):
     levels = len(remote)
     sums_out, stat_out, end_marks, matrices = rest[:4]
     queries_out, mass_out = rest[4 : 4 + levels], rest[4 + levels : 4 + 2 * levels]
@@ -320,6 +315,9 @@
     count = lax.axis_size("seq")
     leaves = tokens // LEAF
     first_leaf = rank * leaves
+    for n in range(leaves):
+        cols = slice(n * LEAF, (n + 1) * LEAF)
+        q_cols[:, cols] = dot(q[...], one_hot(order[:, cols], tokens)).astype(BF16)
     copy.wait()
     near_terms = {}
     for n in range(leaves):
@@ -381,18 +379,31 @@
     matrices[0] = twice
     for j in range(4):
         matrices[j + 1] = spread_matrix(8, j * 32)
-    for block in range(leaves // 2):
-        for h in range(2):
-            coarse = to_spread(results[2, block // 2, h])
-            half = slice((block % 2) * LANES, (block % 2 + 1) * LANES)
-            fine = to_spread(merge([results[1, block, h], spread(coarse[:, half], twice)]))
-            for part in range(2):
-                n = 2 * block + part
-                cols = slice(n * LEAF, (n + 1) * LEAF)
-                term = spread(fine[:, part * LANES : (part + 1) * LANES], twice)
-                if 0 < n < leaves - 1:
-                    term = merge([near_terms[n, h], term])
-                stat_out[h, 0:1, cols], sums_out[h, :, cols], stat_out[h, 1:2, cols] = term
+    coarse = {at: to_spread(results[2, at[0], at[1]]) for at in ((b, h) for b in range(leaves // 4) for h in range(2))}
+    fine = {}
+
+    def join_unit(block, h):
+        half = slice((block % 2) * LANES, (block % 2 + 1) * LANES)
+
+        def second(x):
+            fine[block, h] = to_spread(merge([results[1, block, h], from_spread(x)]))
+
+        return functools.partial(dot, coarse[block // 2, h][:, half], twice), second
+
+    def token_unit(n, h):
+        cols = slice(n * LEAF, (n + 1) * LEAF)
+        half = slice((n % 2) * LANES, (n % 2 + 1) * LANES)
+
+        def second(x):
+            term = from_spread(x)
+            if 0 < n < leaves - 1:
+                term = merge([near_terms[n, h], term])
+            stat_out[h, 0:1, cols], sums_out[h, :, cols], stat_out[h, 1:2, cols] = term
+
+        return (lambda: dot(fine[n // 2, h][:, half], twice)), second
+
+    staggered([join_unit(block, h) for block in range(leaves // 2) for h in range(2)], 4)
+    staggered([token_unit(n, h) for n in range(leaves) for h in range(2)], 4)
 
     row = iota((LEAF, LANES), 0)
     for side, leaf in ((0, first_leaf - 1), (1, first_leaf + leaves)):
@@ -454,10 +465,7 @@
         if index == 0:
             fields = [decode(pair, halo_rows(), rows)]
         else:
-            refs = [(packs[2**index - 2 + i], 0) for i in range(2**index - (index == 1 and joined(tokens, step)))]
-            if index == 1 and joined(tokens, step):
-                refs.append((step, halo_rows()))
-            fields = [decode(ref, at, rows) for ref, at in refs]
+            fields = [decode(packs[2**index - 2 + i], 0, rows) for i in range(2**index)]
         means, sums = [jnp.concatenate(field, axis=1) for field in zip(*fields)]
         keys = far_keys(means, mass_in[index][...])
         values = far_values(sums, mass_in[index][...])
@@ -481,28 +489,34 @@
         for index in reversed(range(levels - 1)):
             rows = level_shape(remote[index], tokens)[1]
             merged = merge(
-                [results[index, h], spread(to_spread(merged)[:, :LANES], matrices[0, :, :rows])]
+                [results[index, h], from_spread(dot(to_spread(merged)[:, :LANES], matrices[0, :, :rows]))]
             )
         coarse.append(to_spread(merged))
     copies = []
-    for n in range(leaves):
+
+    def token_unit(n, h):
         cols = slice(n * LEAF, (n + 1) * LEAF)
         half = slice(n // 4 * LANES, (n // 4 + 1) * LANES)
-        for h in range(2):
+
+        def second(x):
             terms = [
                 (stat_in[h, 0:1, cols], sums_in[h, :, cols], stat_in[h, 1:2, cols]),
-                spread(coarse[h][:, half], matrices[n % 4 + 1]),
+                from_spread(x),
             ]
             if (n, h) in ends:
                 terms.append(ends[n, h])
             _, sums, totals = merge(terms)
             stage[h, :, cols] = (sums * (1.0 / totals)).astype(BF16)
-        if n % 2:
-            both = slice((n - 1) * LEAF, (n + 1) * LEAF)
-            copies.append(
-                pltpu.make_async_copy(stage.at[:, :, both], out.at[:, :, both], sems.at[n // 2])
-            )
-            copies[-1].start()
+            if n % 2 and h:
+                both = slice((n - 1) * LEAF, (n + 1) * LEAF)
+                copies.append(
+                    pltpu.make_async_copy(stage.at[:, :, both], out.at[:, :, both], sems.at[n // 2])
+                )
+                copies[-1].start()
+
+        return functools.partial(dot, coarse[h][:, half], matrices[n % 4 + 1]), second
+
+    staggered([token_unit(n, h) for n in range(leaves) for h in range(2)], 4)
     for copy in copies:
         copy.wait()
 
@@ -513,6 +527,17 @@
 
 def params():
     return pltpu.CompilerParams(vmem_limit_bytes=48 * 2**20)
+
+
+def step_pairs(count, heads):
+    pairs = []
+    for i in range(count):
+        for h in range(heads):
+            if 0 < i < count - 1:
+                pairs.append((i * heads + h, (i + 1 if i % 2 else i - 1) * heads + h))
+            else:
+                pairs.append((i * heads + h, i * heads + (h ^ 1 if heads % 2 == 0 else h)))
+    return pairs
 
 
 def head_pair(q, k, v, order, counts):
@@ -521,65 +546,69 @@
     count = lax.axis_size("seq")
     depth = (tokens * count // LEAF).bit_length() - 1
     remote = tuple(range(leaves.bit_length() - 1, depth))
-    four = False
     flat = (2 * HEAD, tokens)
     shape = jax.ShapeDtypeStruct
+    widths = [level_shape(level, tokens)[1] for level in remote]
+    sent = [shape((pack_rows(i, tokens, level), LANES), SENT) for i, level in enumerate(remote)]
     outs = [
         shape((tokens, 4 * HEAD), BF16),
         shape(flat, BF16),
-        shape(flat, BF16),
-        shape((pack_rows(0, tokens, remote[0]), LANES), SENT),
-        shape((halo_rows() + (pack_rows(1, tokens, remote[1]) if four else 0), LANES), SENT),
-    ] + [shape((pack_rows(i, tokens, remote[i]), LANES), SENT) for i in range(1, len(remote))]
-    counts, order, k, v, q = (
+        shape((1, tokens), jnp.int32),
+        shape((2 * LANES, LEAF), BF16),
+        sent[0],
+    ] + [shape((width, 2 * LANES), F32) for width in widths[1:]]
+    counts, order, k, v = (
         pltpu.with_memory_space_constraint(x, pltpu.HBM)
-        for x in (counts, order, k.reshape(flat), v.reshape(flat), q.reshape(flat))
+        for x in (counts, order, k.reshape(flat), v.reshape(flat))
     )
-    kv_rows, v_cols, q_cols, pair, step, *packs = pl.pallas_call(
-        functools.partial(kv_kernel, tokens, remote),
+    kv_rows, v_cols, order_here, other, pair, *sums = pl.pallas_call(
+        functools.partial(key_kernel, tokens, remote),
         out_shape=outs,
-        in_specs=[ANY] * 5,
+        in_specs=[ANY] * 4,
         out_specs=[VMEM] * len(outs),
         scratch_shapes=[
             pltpu.SMEM(counts.shape, jnp.int32),
-            pltpu.VMEM((1, tokens), jnp.int32),
             pltpu.VMEM(flat, BF16),
             pltpu.VMEM(flat, BF16),
-            pltpu.VMEM(flat, BF16),
-            pltpu.SemaphoreType.DMA((5,)),
+            pltpu.SemaphoreType.DMA((4,)),
         ],
         compiler_params=params(),
         cost_estimate=pl.CostEstimate(
             flops=2 * 256 * tokens * tokens, bytes_accessed=4 * 2**20, transcendentals=0
         ),
         name="gather_keys",
-    )(counts, order, k, v, q)
-
+    )(counts, order, k, v)
     got_pair = lax.ppermute(pair, "seq", [(i, i ^ 1) for i in range(count)])
+
+    outs = [shape((halo_rows(), LANES), SENT)] + sent[1:]
+    step, *packs = pl.pallas_call(
+        functools.partial(pack_kernel, tokens, remote),
+        out_shape=outs,
+        in_specs=[ANY] + [VMEM] * len(remote),
+        out_specs=[VMEM] * len(outs),
+        scratch_shapes=[pltpu.SMEM(counts.shape, jnp.int32), pltpu.SemaphoreType.DMA(())],
+        compiler_params=params(),
+        cost_estimate=pl.CostEstimate(flops=2**20, bytes_accessed=2**18, transcendentals=0),
+        name="pack_rest",
+    )(counts, other, *sums)
     got = []
     for index in range(1, len(remote)):
         for partner in range(2**index, 2 ** (index + 1)):
-            if four and partner == 3:
-                continue
             got.append(
                 lax.ppermute(packs[index - 1], "seq", [(i, i ^ partner) for i in range(count)])
             )
-    swaps = [(i, count - 1 - i) for i in range(count)] if four else []
-    for i in range(1, count - 1, 2):
-        swaps += [] if four else [(i, i + 1), (i + 1, i)]
-    got_step = lax.ppermute(step, "seq", swaps) if swaps else jnp.zeros_like(step)
-
-    widths = [level_shape(level, tokens)[1] for level in remote]
+    got_step = lax.ppermute(step, ("seq", "head"), step_pairs(count, lax.axis_size("head")))
+
     outs = (
-        [shape((2, HEAD, tokens), F32), shape((2, 2, tokens), F32)]
+        [shape(flat, BF16), shape((2, HEAD, tokens), F32), shape((2, 2, tokens), F32)]
         + [shape((2, 3 * LEAF, LANES), BF16), shape((5, LANES, LEAF), BF16)]
         + [shape((2, 2 * HEAD, width), BF16) for width in widths]
         + [shape((16, 2**i * width), F32) for i, width in enumerate(widths)]
     )
-    local = pl.pallas_call(
+    q_cols, *local = pl.pallas_call(
         functools.partial(local_kernel, tokens, remote),
         out_shape=outs,
-        in_specs=[ANY] + [VMEM] * 3,
+        in_specs=[ANY] + [VMEM] * 4,
         out_specs=[VMEM] * len(outs),
         scratch_shapes=[
             pltpu.SMEM(counts.shape, jnp.int32),
@@ -587,9 +616,9 @@
             pltpu.VMEM((tokens, LANES), BF16),
         ],
         compiler_params=params(),
-        cost_estimate=pl.CostEstimate(flops=2**33, bytes_accessed=8 * 2**20, transcendentals=2**22),
+        cost_estimate=pl.CostEstimate(flops=2**20, bytes_accessed=2**16, transcendentals=0),
         name="local_attention",
-    )(counts, q_cols, kv_rows, v_cols)
+    )(counts, q.reshape(flat), order_here, kv_rows, v_cols)
     return pl.pallas_call(
         functools.partial(last_kernel, tokens, remote),
         out_shape=shape((2, HEAD, tokens), BF16),

time: 26.9 us -> 23.2 us (0.86)
  starting transfers between devices: 10.6 us -> 7.76 us
  Pallas kernels: 16 us -> 15.2 us
    ppermute x1, starting transfers between devices: 4.79 us -> 3.09 us  [head_pair(): got_pair = lax.ppermute(pair, 'seq', [(i, i ^ 1) for i in range(count)])]
    pallas_call x1 -> x2, Pallas kernels: 5.45 us -> 4.86 us  [the longest x1 4.05 us: head_pair(): pl.pallas_call(functools.partial(key_kernel, tokens, remote), out_shape=o...]
    ppermute x1, starting transfers between devices: 0.66 us -> 0.07 us  [head_pair(): lax.ppermute(step, ('seq', 'head'), step_pairs(count, lax.axis_size('head...]
    ppermute x2, starting transfers between devices: 5.11 us -> 4.6 us  [head_pair(): lax.ppermute(packs[index - 1], 'seq', [(i, i ^ partner) for i in range(co...]
  transfers between devices with their start and end apart: 4 -> 4, of which waited for: 0 -> 1; matrix products, arithmetic and copies ran while one was open for 0% -> 0% of each run, Pallas kernels for 28% -> 35%
where the time goes in v2:
time: 23.2 us; the launch traced here: 23.1 us
  Pallas kernels  15.2 us (66%)
  starting transfers between devices  7.76 us (33%)
    pallas_call x1, Pallas kernels, head_pair(): pl.pallas_call(functools.partial(local_kernel, tokens, remote), out_shape...  7.26 us
    ppermute x2, starting transfers between devices, head_pair(): lax.ppermute(packs[index - 1], 'seq', [(i, i ^ partner) for i in range(co...  4.6 us
    pallas_call x1, Pallas kernels, head_pair(): pl.pallas_call(functools.partial(key_kernel, tokens, remote), out_shape=o...  4.05 us
    ppermute x1, starting transfers between devices, head_pair(): got_pair = lax.ppermute(pair, 'seq', [(i, i ^ 1) for i in range(count)])  3.09 us
    pallas_call x1, Pallas kernels, head_pair(): pl.pallas_call(functools.partial(last_kernel, tokens, remote), out_shape=...  3.06 us
    pallas_call x1, Pallas kernels, head_pair(): pl.pallas_call(functools.partial(pack_kernel, tokens, remote), out_shape=...  0.81 us
  transfers between devices with their start and end apart: 4, of which 1 were waited for; matrix products, arithmetic and copies ran while one was open for 0% of the time, Pallas kernels for 35%

profile of v2, /device:TPU:0, one launch (start us, length us, event | category | flops | bytes accessed | tf_op | source)
XLA Modules:
  0.0 23.1 jit_solution(592040489964071507)
XLA Ops:
  0.0 0.0 copy-start
  0.0 4.0 %gather_keys.1 = (bf16[2048,256]{1,0:T(8,128)(2,1)S(1)}, bf16[128,2048]{1,0:T(8,128)(2,1)S(1)}, s32[1,2048]{1,0:T(1,128)S(1)}, bf16[256,256]{1,0:T(8,128)(2,1)S(...) custom-call(s32[32]{0:T(128)} %counts_in.5, s32[1,2048]{1,0:T(1,128)} %order_in.1, bf16[128,2048]{1,0:T(8,128)(2,1)} %bitcast.4, ...), custom_call_target="tpu_custom_call" | custom-call | flops 2147483648 | bytes 4194304 | tf_op jit(solution)/shard_map/gather_keys/pallas_call | solution.py:564
  4.1 3.1 %collective-permute-start = (s16[1088,128]{1,0:T(8,128)(2,1)S(1)}, s16[1088,128]{1,0:T(8,128)(2,1)S(1)}, u32[]{:S(2)}, u32[]{:S(2)}) collective-permute-start(s16[1088,128]{1,0:T(8,128)(2,1)S(1)} %get-tuple-element.34), channel_id=1, source_target_pairs={{0,4},{4,0},{8,12},{12,8},{1,5},{5,1},{9,13},{13,9},{2,6},{6,2},{1... | collective-permute-start | bytes 835592 | tf_op jit(solution)/shard_map/ppermute | solution.py:581
  7.1 0.8 %pack_rest.1 = (s16[544,128]{1,0:T(8,128)(2,1)S(1)}, s16[272,128]{1,0:T(8,128)(2,1)S(1)}) custom-call(s32[32]{0:T(128)} %counts_in.5, bf16[256,256]{1,0:T(8,128)(2,1)S(1)} %get-tuple-element.35.other, f32[128,256]{1,0:T(8,128)S(1)} %get-tuple-element.36.rest_0_), custom_call_target="tpu_custom_call" | custom-call | flops 1048576 | bytes 262144 | tf_op jit(solution)/shard_map/pack_rest/pallas_call | solution.py:584
  8.0 0.1 collective-permute-start.1
  8.0 2.5 %collective-permute-start.3 = (s16[272,128]{1,0:T(8,128)(2,1)S(1)}, s16[272,128]{1,0:T(8,128)(2,1)S(1)}, u32[]{:S(2)}, u32[]{:S(2)}) collective-permute-start(s16[272,128]{1,0:T(8,128)(2,1)S(1)} %get-tuple-element.38), channel_id=1, source_target_pairs={{0,12},{4,8},{8,4},{12,0},{1,13},{5,9},{9,5},{13,1},{2,14},{6,10},... | collective-permute-start | bytes 208904 | tf_op jit(solution)/shard_map/ppermute | solution.py:598
  10.6 2.1 %collective-permute-start.2 = (s16[272,128]{1,0:T(8,128)(2,1)S(1)}, s16[272,128]{1,0:T(8,128)(2,1)S(1)}, u32[]{:S(2)}, u32[]{:S(2)}) collective-permute-start(s16[272,128]{1,0:T(8,128)(2,1)S(1)} %get-tuple-element.38), channel_id=1, source_target_pairs={{0,8},{4,12},{8,0},{12,4},{1,9},{5,13},{9,1},{13,5},{2,10},{6,14},... | collective-permute-start | bytes 208904 | tf_op jit(solution)/shard_map/ppermute | solution.py:598
  12.6 0.0 copy-done
  12.6 7.3 %local_attention.1 = (bf16[128,2048]{1,0:T(8,128)(2,1)S(1)}, f32[2,64,2048]{2,1,0:T(8,128)S(1)}, f32[2,2,2048]{2,1,0:T(2,128)S(1)}, bf16[2,768,128]{2,1,0:T(8,12...) custom-call(s32[32]{0:T(128)} %counts_in.5, ...), custom_call_target="tpu_custom_call" | custom-call | flops 1048576 | bytes 65536 | tf_op jit(solution)/shard_map/local_attention/pallas_call | solution.py:608
  19.9 0.0 collective-permute-done.3.rest_7_
  19.9 0.1 collective-permute-done.2.rest_6_
  20.0 0.0 collective-permute-done.1.rest_5_
  20.0 0.0 collective-permute-done.rest_4_
  20.0 3.1 %remote_attention.1 = bf16[2,64,2048]{2,1,0:T(8,128)(2,1)} custom-call(bf16[128,2048]{1,0:T(8,128)(2,1)S(1)} %get-tuple-element.25.q_cols, bf16[2048,256]{1,0:T(8,128)(2,1)S(1)} %get-tuple-element.23.kv_rows, bf16[128,2048]{1,0:T(8,128)(2,1)S(1)} %get-tuple-element.24.v_cols, f32[2,64,2048]{2,1,0:T(8,128)S(1)} %get-tuple-element.26.sums_in, ...), custom_call_target="tpu_custom_call" | custom-call | flops 1073741824 | bytes 4194304 | tf_op jit(solution)/shard_map/remote_attention/pallas_call | solution.py:622
Async XLA Ops:
  0.0 12.6 %copy-start = (bf16[2,64,2048]{2,1,0:T(8,128)(2,1)S(1)}, bf16[2,64,2048]{2,1,0:T(8,128)(2,1)}, u32[]{:S(2)}) copy-start(bf16[2,64,2048]{2,1,0:T(8,128)(2,1)} %param.5) | copy-start | bytes 1572868
  4.1 15.9 %collective-permute-start = (s16[1088,128]{1,0:T(8,128)(2,1)S(1)}, s16[1088,128]{1,0:T(8,128)(2,1)S(1)}, u32[]{:S(2)}, u32[]{:S(2)}) collective-permute-start(s16[1088,128]{1,0:T(8,128)(2,1)S(1)} %get-tuple-element.34), channel_id=1, source_target_pairs={{0,4},{4,0},{8,12},{12,8},{1,5},{5,1},{9,13},{13,9},{2,6},{6,2},{1... | collective-permute-start | bytes 835592 | tf_op jit(solution)/shard_map/ppermute | solution.py:581
  8.0 12.0 %collective-permute-start.1 = (s16[544,128]{1,0:T(8,128)(2,1)S(1)}, s16[544,128]{1,0:T(8,128)(2,1)S(1)}, u32[]{:S(2)}, u32[]{:S(2)}) collective-permute-start(s16[544,128]{1,0:T(8,128)(2,1)S(1)} %get-tuple-element.37), channel_id=1, source_target_pairs={{0,1},{1,0},{2,3},{3,2},{4,8},{5,9},{6,10},{7,11},{8,4},{9,5},{10,... | collective-permute-start | bytes 417800 | tf_op jit(solution)/shard_map/ppermute | solution.py:600
  8.0 11.9 %collective-permute-start.3 = (s16[272,128]{1,0:T(8,128)(2,1)S(1)}, s16[272,128]{1,0:T(8,128)(2,1)S(1)}, u32[]{:S(2)}, u32[]{:S(2)}) collective-permute-start(s16[272,128]{1,0:T(8,128)(2,1)S(1)} %get-tuple-element.38), channel_id=1, source_target_pairs={{0,12},{4,8},{8,4},{12,0},{1,13},{5,9},{9,5},{13,1},{2,14},{6,10},... | collective-permute-start | bytes 208904 | tf_op jit(solution)/shard_map/ppermute | solution.py:598
  10.6 9.4 %collective-permute-start.2 = (s16[272,128]{1,0:T(8,128)(2,1)S(1)}, s16[272,128]{1,0:T(8,128)(2,1)S(1)}, u32[]{:S(2)}, u32[]{:S(2)}) collective-permute-start(s16[272,128]{1,0:T(8,128)(2,1)S(1)} %get-tuple-element.38), channel_id=1, source_target_pairs={{0,8},{4,12},{8,0},{12,4},{1,9},{5,13},{9,1},{13,5},{2,10},{6,14},... | collective-permute-start | bytes 208904 | tf_op jit(solution)/shard_map/ppermute | solution.py:598

commit v3 on v2

--- a/solution.py
+++ b/solution.py
@@ -90,28 +90,34 @@
     return (leaf * per_leaf) // rows, (leaf * per_leaf) % rows
 
 
-def pooled(levels, leaf_values, tokens):
-    sums = {}
-    whole = [level for level in levels if LEAF // 2**level % 16 == 0]
-    parts = [pool_rows(2**level, 0, LEAF // 2**level) for level in whole]
-    for leaf, values in enumerate(leaf_values):
-        both = dot(jnp.concatenate(parts, axis=0), values)
+class Pool:
+    def __init__(self, levels, tokens):
+        self.levels, self.tokens = levels, tokens
+        self.whole = [level for level in levels if LEAF // 2**level % 16 == 0]
+        parts = [pool_rows(2**level, 0, LEAF // 2**level) for level in self.whole]
+        self.matrix = jnp.concatenate(parts, axis=0) if parts else None
+        self.pieces, self.sums = {}, {}
+
+    def add(self, leaf, values):
+        both = dot(self.matrix, values) if self.whole else None
         at = 0
-        for level in whole:
-            count = LEAF // 2**level
-            block, _ = place(level, leaf, tokens)
-            sums.setdefault((level, block), []).append(both[at : at + count])
-            at += count
-    out = {at: jnp.concatenate(pieces, axis=0) for at, pieces in sums.items()}
-    for level in levels:
-        if level in whole:
-            continue
-        group, rows, _ = level_shape(level, tokens)
-        for leaf, values in enumerate(leaf_values):
-            block, first = place(level, leaf, tokens)
-            piece = dot(pool_rows(group, first, rows), values)
-            out[level, block] = out[level, block] + piece if leaf else piece
-    return out
+        for level in self.levels:
+            block, first = place(level, leaf, self.tokens)
+            if level in self.whole:
+                count = LEAF // 2**level
+                self.pieces.setdefault((level, block), {})[leaf] = both[at : at + count]
+                at += count
+            else:
+                group, rows, _ = level_shape(level, self.tokens)
+                piece = dot(pool_rows(group, first, rows), values)
+                old = self.sums.get((level, block))
+                self.sums[level, block] = piece if old is None else old + piece
+
+    def get(self, level, block):
+        if level not in self.whole:
+            return self.sums[level, block]
+        pieces = self.pieces[level, block]
+        return jnp.concatenate([pieces[leaf] for leaf in sorted(pieces)], axis=0)
 
 
 def mass(counts, first_leaf, leaves, group, rows):
@@ -262,46 +268,53 @@
     for copy in copies[1:]:
         copy.wait()
     joint = jnp.concatenate([k[...], v[...]], axis=0)
-    masked = []
-    got = []
-    for n in range(leaves):
-        cols = slice(n * LEAF, (n + 1) * LEAF)
-        got.append(dot(joint, one_hot(order[:, cols], tokens) if n else first).astype(BF16))
+    odd = jnp.where(rank % 2 == 1, 1, 0)
+    pool = Pool(remote, tokens)
+    got = {}
+    masked = {}
+
+    def after(n):
+        cols = slice(n * LEAF, (n + 1) * LEAF)
         rows = got[n].T
         kv_rows[cols, :] = rows
         v_cols[:, cols] = got[n][LANES:]
-        masked.append(valid_only(rows, counts[rank * leaves + n]))
-    odd = jnp.where(rank % 2 == 1, 1, 0)
-    low, high = got[0].astype(F32), got[-1].astype(F32)
-    halo = jnp.where(odd == 1, low, high)
-    put(pair, 0, encode(halo[:LANES], halo[LANES:]))
-    other[...] = jnp.where(odd == 1, high, low).astype(BF16)
-    sums = pooled(remote, masked, tokens)
-    put(pair, halo_rows(), coarse_codes(counts, rank, remote[0], sums[remote[0], 0], tokens))
+        masked[n] = valid_only(rows, counts[rank * leaves + n])
+
+    def halos():
+        low, high = got[0].astype(F32), got[leaves - 1].astype(F32)
+        halo = jnp.where(odd == 1, low, high)
+        put(pair, 0, encode(halo[:LANES], halo[LANES:]))
+        other[...] = jnp.where(odd == 1, high, low).astype(BF16)
+
+    for n in range(leaves):
+        cols = slice(n * LEAF, (n + 1) * LEAF)
+        got[n] = dot(joint, one_hot(order[:, cols], tokens) if n else first).astype(BF16)
+        after(n)
+    halos()
+    for n in range(leaves):
+        pool.add(n, masked[n])
+    put(pair, halo_rows(), encode(*coarse_parts(counts, rank, remote[0], pool, tokens)))
     for ref, level in zip(sums_out, remote[1:]):
-        ref[...] = sums[level, 0]
-
-
-def pack_kernel(tokens, remote, counts_in, other, *rest):
-    levels = len(remote) - 1
-    sums, step, packs = rest[:levels], rest[levels], rest[levels + 1 : 2 * levels + 1]
-    counts, sem = rest[2 * levels + 1 :]
-    copy = pltpu.make_async_copy(counts_in, counts, sem)
-    copy.start()
-    rank = lax.axis_index("seq")
+        means, sums = coarse_parts(counts, rank, level, pool, tokens)
+        ref[:LANES, :] = means
+        ref[LANES:, :] = sums
+
+
+def pack_kernel(other, *rest):
+    levels = len(rest) // 2
+    sums, step, packs = rest[:levels], rest[levels], rest[levels + 1 :]
     halo = other[...].astype(F32)
     put(step, 0, encode(halo[:LANES], halo[LANES:]))
-    copy.wait()
-    for i, level in enumerate(remote[1:]):
-        put(packs[i], 0, coarse_codes(counts, rank, level, sums[i][...], tokens))
-
-
-def coarse_codes(counts, rank, level, sums, tokens):
+    for ref, x in zip(packs, sums):
+        put(ref, 0, encode(x[:LANES, :], x[LANES:, :]))
+
+
+def coarse_parts(counts, rank, level, pool, tokens):
     group, rows, _ = level_shape(level, tokens)
     leaves = tokens // LEAF
     weight = mass(counts, rank * leaves, leaves, group, rows)[:1]
-    sums = sums.T
-    return encode(sums[:LANES] / jnp.maximum(weight, 1.0), sums[LANES:])
+    sums = pool.get(level, 0).T
+    return sums[:LANES] / jnp.maximum(weight, 1.0), sums[LANES:]
 
 
 def local_kernel(tokens, remote, counts_in, q, order, kv_rows, v_cols, q_cols, *rest):
@@ -315,11 +328,14 @@
     count = lax.axis_size("seq")
     leaves = tokens // LEAF
     first_leaf = rank * leaves
+    near_terms = {}
+    q_pool = Pool((1, 2) + tuple(remote), tokens)
+    kv_pool = Pool((1, 2), tokens)
     for n in range(leaves):
         cols = slice(n * LEAF, (n + 1) * LEAF)
-        q_cols[:, cols] = dot(q[...], one_hot(order[:, cols], tokens)).astype(BF16)
+        got = dot(q[...], one_hot(order[:, cols], tokens)).astype(BF16)
+        q_cols[:, cols] = got
     copy.wait()
-    near_terms = {}
     for n in range(leaves):
         rows = slice(n * LEAF, (n + 1) * LEAF)
         mark[rows, :] = near_marks(iota((LEAF, LANES), 0) >= counts[first_leaf + n])
@@ -338,21 +354,20 @@
         return first, second
 
     staggered([near_unit(n) for n in range(1, leaves - 1)])
-    leaf_q = [q_cols[:, n * LEAF : (n + 1) * LEAF].T for n in range(leaves)]
-    q_sums = pooled((1, 2) + tuple(remote), leaf_q, tokens)
+    for n in range(leaves):
+        cols = slice(n * LEAF, (n + 1) * LEAF)
+        q_pool.add(n, q_cols[:, cols].T)
+    for n in range(leaves):
+        cols = slice(n * LEAF, (n + 1) * LEAF)
+        kv_pool.add(n, valid_only(kv_rows[cols, :], counts[first_leaf + n]))
 
     def queries(level, block):
-        hi, lo = split(q_sums[level, block].T * (SCALE / 2**level))
+        hi, lo = split(q_pool.get(level, block).T * (SCALE / 2**level))
         return [
             jnp.concatenate([x[h * HEAD : (h + 1) * HEAD] for x in (hi, lo)], axis=0)
             for h in range(2)
         ]
 
-    masked = [
-        valid_only(kv_rows[n * LEAF : (n + 1) * LEAF, :], counts[first_leaf + n])
-        for n in range(leaves)
-    ]
-    kv_sums = pooled((1, 2), masked, tokens)
     results = {}
     units = []
     for level in (2, 1):
@@ -360,7 +375,7 @@
         per_block = rows * group // LEAF
         for block in range(blocks):
             weight = mass(counts, first_leaf + block * per_block, per_block, group, rows)
-            sums = kv_sums[level, block].T
+            sums = kv_pool.get(level, block).T
             keys = far_keys(sums[:LANES] / jnp.maximum(weight[:1], 1.0), weight)
             values = far_values(sums[LANES:], weight)
             query = queries(level, block ^ 1)
@@ -556,7 +571,7 @@
         shape((1, tokens), jnp.int32),
         shape((2 * LANES, LEAF), BF16),
         sent[0],
-    ] + [shape((width, 2 * LANES), F32) for width in widths[1:]]
+    ] + [shape((2 * LANES, width), F32) for width in widths[1:]]
     counts, order, k, v = (
         pltpu.with_memory_space_constraint(x, pltpu.HBM)
         for x in (counts, order, k.reshape(flat), v.reshape(flat))
@@ -582,15 +597,14 @@
 
     outs = [shape((halo_rows(), LANES), SENT)] + sent[1:]
     step, *packs = pl.pallas_call(
-        functools.partial(pack_kernel, tokens, remote),
+        pack_kernel,
         out_shape=outs,
-        in_specs=[ANY] + [VMEM] * len(remote),
+        in_specs=[VMEM] * len(remote),
         out_specs=[VMEM] * len(outs),
-        scratch_shapes=[pltpu.SMEM(counts.shape, jnp.int32), pltpu.SemaphoreType.DMA(())],
         compiler_params=params(),
         cost_estimate=pl.CostEstimate(flops=2**20, bytes_accessed=2**18, transcendentals=0),
         name="pack_rest",
-    )(counts, other, *sums)
+    )(other, *sums)
     got = []
     for index in range(1, len(remote)):
         for partner in range(2**index, 2 ** (index + 1)):

time: 23.2 us -> 22.4 us (0.966)
  Pallas kernels: 15.2 us -> 14.5 us
    pallas_call x1, Pallas kernels: 0.81 us -> 0.09 us  [head_pair(): pl.pallas_call(pack_kernel, out_shape=outs, in_specs=[VMEM] * len(remote)...]
  transfers between devices with their start and end apart: 4 -> 4, of which waited for: 1 -> 0; matrix products, arithmetic and copies ran while one was open for 0% -> 0% of each run, Pallas kernels for 35% -> 33%
where the time goes in v3:
time: 22.4 us; the launch traced here: 22.3 us
  Pallas kernels  14.5 us (65%)
  starting transfers between devices  7.76 us (35%)
    pallas_call x1, Pallas kernels, head_pair(): pl.pallas_call(functools.partial(local_kernel, tokens, remote), out_shape...  7.29 us
    ppermute x2, starting transfers between devices, head_pair(): lax.ppermute(packs[index - 1], 'seq', [(i, i ^ partner) for i in range(co...  4.6 us
    pallas_call x1, Pallas kernels, head_pair(): pl.pallas_call(functools.partial(key_kernel, tokens, remote), out_shape=o...  4.02 us
    ppermute x1, starting transfers between devices, head_pair(): got_pair = lax.ppermute(pair, 'seq', [(i, i ^ 1) for i in range(count)])  3.09 us
    pallas_call x1, Pallas kernels, head_pair(): pl.pallas_call(functools.partial(last_kernel, tokens, remote), out_shape=...  3.07 us
  transfers between devices with their start and end apart: 4, of which 0 were waited for; matrix products, arithmetic and copies ran while one was open for 0% of the time, Pallas kernels for 33%

profile of v3, /device:TPU:0, one launch (start us, length us, event | category | flops | bytes accessed | tf_op | source)
XLA Modules:
  0.0 22.3 jit_solution(7360002782726332848)
XLA Ops:
  0.0 0.0 copy-start
  0.0 4.0 %gather_keys.1 = (bf16[2048,256]{1,0:T(8,128)(2,1)S(1)}, bf16[128,2048]{1,0:T(8,128)(2,1)S(1)}, s32[1,2048]{1,0:T(1,128)S(1)}, bf16[256,256]{1,0:T(8,128)(2,1)S(...) custom-call(s32[32]{0:T(128)} %counts_in.3, s32[1,2048]{1,0:T(1,128)} %order_in.1, bf16[128,2048]{1,0:T(8,128)(2,1)} %bitcast.4, ...), custom_call_target="tpu_custom_call" | custom-call | flops 2147483648 | bytes 4194304 | tf_op jit(solution)/shard_map/gather_keys/pallas_call | solution.py:579
  4.0 3.1 %collective-permute-start = (s16[1088,128]{1,0:T(8,128)(2,1)S(1)}, s16[1088,128]{1,0:T(8,128)(2,1)S(1)}, u32[]{:S(2)}, u32[]{:S(2)}) collective-permute-start(s16[1088,128]{1,0:T(8,128)(2,1)S(1)} %get-tuple-element.34), channel_id=1, source_target_pairs={{0,4},{4,0},{8,12},{12,8},{1,5},{5,1},{9,13},{13,9},{2,6},{6,2},{1... | collective-permute-start | bytes 835592 | tf_op jit(solution)/shard_map/ppermute | solution.py:596
  7.1 0.1 pack_rest.1
  7.2 0.1 collective-permute-start.1
  7.3 2.5 %collective-permute-start.3 = (s16[272,128]{1,0:T(8,128)(2,1)S(1)}, s16[272,128]{1,0:T(8,128)(2,1)S(1)}, u32[]{:S(2)}, u32[]{:S(2)}) collective-permute-start(s16[272,128]{1,0:T(8,128)(2,1)S(1)} %get-tuple-element.38), channel_id=1, source_target_pairs={{0,12},{4,8},{8,4},{12,0},{1,13},{5,9},{9,5},{13,1},{2,14},{6,10},... | collective-permute-start | bytes 208904 | tf_op jit(solution)/shard_map/ppermute | solution.py:612
  9.8 2.1 %collective-permute-start.2 = (s16[272,128]{1,0:T(8,128)(2,1)S(1)}, s16[272,128]{1,0:T(8,128)(2,1)S(1)}, u32[]{:S(2)}, u32[]{:S(2)}) collective-permute-start(s16[272,128]{1,0:T(8,128)(2,1)S(1)} %get-tuple-element.38), channel_id=1, source_target_pairs={{0,8},{4,12},{8,0},{12,4},{1,9},{5,13},{9,1},{13,5},{2,10},{6,14},... | collective-permute-start | bytes 208904 | tf_op jit(solution)/shard_map/ppermute | solution.py:612
  11.9 0.0 copy-done
  11.9 7.3 %local_attention.1 = (bf16[128,2048]{1,0:T(8,128)(2,1)S(1)}, f32[2,64,2048]{2,1,0:T(8,128)S(1)}, f32[2,2,2048]{2,1,0:T(2,128)S(1)}, bf16[2,768,128]{2,1,0:T(8,12...) custom-call(s32[32]{0:T(128)} %counts_in.3, ...), custom_call_target="tpu_custom_call" | custom-call | flops 1048576 | bytes 65536 | tf_op jit(solution)/shard_map/local_attention/pallas_call | solution.py:622
  19.2 0.0 collective-permute-done.3.rest_7_
  19.2 0.0 collective-permute-done.2.rest_6_
  19.2 0.0 collective-permute-done.1.rest_5_
  19.2 0.0 collective-permute-done.rest_4_
  19.2 3.1 %remote_attention.1 = bf16[2,64,2048]{2,1,0:T(8,128)(2,1)} custom-call(bf16[128,2048]{1,0:T(8,128)(2,1)S(1)} %get-tuple-element.25.q_cols, bf16[2048,256]{1,0:T(8,128)(2,1)S(1)} %get-tuple-element.23.kv_rows, bf16[128,2048]{1,0:T(8,128)(2,1)S(1)} %get-tuple-element.24.v_cols, f32[2,64,2048]{2,1,0:T(8,128)S(1)} %get-tuple-element.26.sums_in, ...), custom_call_target="tpu_custom_call" | custom-call | flops 1073741824 | bytes 4194304 | tf_op jit(solution)/shard_map/remote_attention/pallas_call | solution.py:636
Async XLA Ops:
  0.0 11.9 %copy-start = (bf16[2,64,2048]{2,1,0:T(8,128)(2,1)S(1)}, bf16[2,64,2048]{2,1,0:T(8,128)(2,1)}, u32[]{:S(2)}) copy-start(bf16[2,64,2048]{2,1,0:T(8,128)(2,1)} %param.5) | copy-start | bytes 1572868
  4.0 15.2 %collective-permute-start = (s16[1088,128]{1,0:T(8,128)(2,1)S(1)}, s16[1088,128]{1,0:T(8,128)(2,1)S(1)}, u32[]{:S(2)}, u32[]{:S(2)}) collective-permute-start(s16[1088,128]{1,0:T(8,128)(2,1)S(1)} %get-tuple-element.34), channel_id=1, source_target_pairs={{0,4},{4,0},{8,12},{12,8},{1,5},{5,1},{9,13},{13,9},{2,6},{6,2},{1... | collective-permute-start | bytes 835592 | tf_op jit(solution)/shard_map/ppermute | solution.py:596
  7.2 12.0 %collective-permute-start.1 = (s16[544,128]{1,0:T(8,128)(2,1)S(1)}, s16[544,128]{1,0:T(8,128)(2,1)S(1)}, u32[]{:S(2)}, u32[]{:S(2)}) collective-permute-start(s16[544,128]{1,0:T(8,128)(2,1)S(1)} %get-tuple-element.37), channel_id=1, source_target_pairs={{0,1},{1,0},{2,3},{3,2},{4,8},{5,9},{6,10},{7,11},{8,4},{9,5},{10,... | collective-permute-start | bytes 417800 | tf_op jit(solution)/shard_map/ppermute | solution.py:614
  7.3 11.9 %collective-permute-start.3 = (s16[272,128]{1,0:T(8,128)(2,1)S(1)}, s16[272,128]{1,0:T(8,128)(2,1)S(1)}, u32[]{:S(2)}, u32[]{:S(2)}) collective-permute-start(s16[272,128]{1,0:T(8,128)(2,1)S(1)} %get-tuple-element.38), channel_id=1, source_target_pairs={{0,12},{4,8},{8,4},{12,0},{1,13},{5,9},{9,5},{13,1},{2,14},{6,10},... | collective-permute-start | bytes 208904 | tf_op jit(solution)/shard_map/ppermute | solution.py:612
  9.8 9.4 %collective-permute-start.2 = (s16[272,128]{1,0:T(8,128)(2,1)S(1)}, s16[272,128]{1,0:T(8,128)(2,1)S(1)}, u32[]{:S(2)}, u32[]{:S(2)}) collective-permute-start(s16[272,128]{1,0:T(8,128)(2,1)S(1)} %get-tuple-element.38), channel_id=1, source_target_pairs={{0,8},{4,12},{8,0},{12,4},{1,9},{5,13},{9,1},{13,5},{2,10},{6,14},... | collective-permute-start | bytes 208904 | tf_op jit(solution)/shard_map/ppermute | solution.py:612

commit v4 on v3

--- a/solution.py
+++ b/solution.py
@@ -493,10 +493,10 @@
             units.append((functools.partial(far_scores, keys[h], queries[index][h]), second))
         return units
 
-    units = [near_unit(0), near_unit(1)]
-    for index in range(levels):
+    units = []
+    for index in reversed(range(levels)):
         units += far_units(index)
-    staggered(units, 2)
+    staggered(units + [near_unit(0), near_unit(1)], 2)
 
     coarse = []
     for h in range(2):

time: 22.4 us -> 22.2 us (level)
  no operation moved by 1% of the time
where the time goes in v4:
time: 22.2 us; the launch traced here: 22.1 us
  Pallas kernels  14.3 us (64%)
  starting transfers between devices  7.76 us (35%)
    pallas_call x1, Pallas kernels, head_pair(): pl.pallas_call(functools.partial(local_kernel, tokens, remote), out_shape...  7.29 us
    ppermute x2, starting transfers between devices, head_pair(): lax.ppermute(packs[index - 1], 'seq', [(i, i ^ partner) for i in range(co...  4.6 us
    pallas_call x1, Pallas kernels, head_pair(): pl.pallas_call(functools.partial(key_kernel, tokens, remote), out_shape=o...  4.02 us
    ppermute x1, starting transfers between devices, head_pair(): got_pair = lax.ppermute(pair, 'seq', [(i, i ^ 1) for i in range(count)])  3.09 us
    pallas_call x1, Pallas kernels, head_pair(): pl.pallas_call(functools.partial(last_kernel, tokens, remote), out_shape=...  2.86 us
  transfers between devices with their start and end apart: 4, of which 0 were waited for; matrix products, arithmetic and copies ran while one was open for 0% of the time, Pallas kernels for 33%

profile of v4, /device:TPU:0, one launch (start us, length us, event | category | flops | bytes accessed | tf_op | source)
XLA Modules:
  0.0 22.1 jit_solution(5464555526023526440)
XLA Ops:
  0.0 0.0 copy-start
  0.0 4.0 %gather_keys.1 = (bf16[2048,256]{1,0:T(8,128)(2,1)S(1)}, bf16[128,2048]{1,0:T(8,128)(2,1)S(1)}, s32[1,2048]{1,0:T(1,128)S(1)}, bf16[256,256]{1,0:T(8,128)(2,1)S(...) custom-call(s32[32]{0:T(128)} %counts_in.3, s32[1,2048]{1,0:T(1,128)} %order_in.1, bf16[128,2048]{1,0:T(8,128)(2,1)} %bitcast.4, ...), custom_call_target="tpu_custom_call" | custom-call | flops 2147483648 | bytes 4194304 | tf_op jit(solution)/shard_map/gather_keys/pallas_call | solution.py:579
  4.0 3.1 %collective-permute-start = (s16[1088,128]{1,0:T(8,128)(2,1)S(1)}, s16[1088,128]{1,0:T(8,128)(2,1)S(1)}, u32[]{:S(2)}, u32[]{:S(2)}) collective-permute-start(s16[1088,128]{1,0:T(8,128)(2,1)S(1)} %get-tuple-element.34), channel_id=1, source_target_pairs={{0,4},{4,0},{8,12},{12,8},{1,5},{5,1},{9,13},{13,9},{2,6},{6,2},{1... | collective-permute-start | bytes 835592 | tf_op jit(solution)/shard_map/ppermute | solution.py:596
  7.1 0.1 pack_rest.1
  7.2 0.1 collective-permute-start.1
  7.3 2.5 %collective-permute-start.3 = (s16[272,128]{1,0:T(8,128)(2,1)S(1)}, s16[272,128]{1,0:T(8,128)(2,1)S(1)}, u32[]{:S(2)}, u32[]{:S(2)}) collective-permute-start(s16[272,128]{1,0:T(8,128)(2,1)S(1)} %get-tuple-element.38), channel_id=1, source_target_pairs={{0,12},{4,8},{8,4},{12,0},{1,13},{5,9},{9,5},{13,1},{2,14},{6,10},... | collective-permute-start | bytes 208904 | tf_op jit(solution)/shard_map/ppermute | solution.py:612
  9.8 2.1 %collective-permute-start.2 = (s16[272,128]{1,0:T(8,128)(2,1)S(1)}, s16[272,128]{1,0:T(8,128)(2,1)S(1)}, u32[]{:S(2)}, u32[]{:S(2)}) collective-permute-start(s16[272,128]{1,0:T(8,128)(2,1)S(1)} %get-tuple-element.38), channel_id=1, source_target_pairs={{0,8},{4,12},{8,0},{12,4},{1,9},{5,13},{9,1},{13,5},{2,10},{6,14},... | collective-permute-start | bytes 208904 | tf_op jit(solution)/shard_map/ppermute | solution.py:612
  11.9 0.0 copy-done
  11.9 7.3 %local_attention.1 = (bf16[128,2048]{1,0:T(8,128)(2,1)S(1)}, f32[2,64,2048]{2,1,0:T(8,128)S(1)}, f32[2,2,2048]{2,1,0:T(2,128)S(1)}, bf16[2,768,128]{2,1,0:T(8,12...) custom-call(s32[32]{0:T(128)} %counts_in.3, ...), custom_call_target="tpu_custom_call" | custom-call | flops 1048576 | bytes 65536 | tf_op jit(solution)/shard_map/local_attention/pallas_call | solution.py:622
  19.2 0.0 collective-permute-done.3.rest_7_
  19.2 0.0 collective-permute-done.2.rest_6_
  19.2 0.0 collective-permute-done.1.rest_5_
  19.2 0.0 collective-permute-done.rest_4_
  19.2 2.9 %remote_attention.1 = bf16[2,64,2048]{2,1,0:T(8,128)(2,1)} custom-call(bf16[128,2048]{1,0:T(8,128)(2,1)S(1)} %get-tuple-element.25.q_cols, bf16[2048,256]{1,0:T(8,128)(2,1)S(1)} %get-tuple-element.23.kv_rows, bf16[128,2048]{1,0:T(8,128)(2,1)S(1)} %get-tuple-element.24.v_cols, f32[2,64,2048]{2,1,0:T(8,128)S(1)} %get-tuple-element.26.sums_in, ...), custom_call_target="tpu_custom_call" | custom-call | flops 1073741824 | bytes 4194304 | tf_op jit(solution)/shard_map/remote_attention/pallas_call | solution.py:636
Async XLA Ops:
  0.0 11.9 %copy-start = (bf16[2,64,2048]{2,1,0:T(8,128)(2,1)S(1)}, bf16[2,64,2048]{2,1,0:T(8,128)(2,1)}, u32[]{:S(2)}) copy-start(bf16[2,64,2048]{2,1,0:T(8,128)(2,1)} %param.5) | copy-start | bytes 1572868
  4.0 15.2 %collective-permute-start = (s16[1088,128]{1,0:T(8,128)(2,1)S(1)}, s16[1088,128]{1,0:T(8,128)(2,1)S(1)}, u32[]{:S(2)}, u32[]{:S(2)}) collective-permute-start(s16[1088,128]{1,0:T(8,128)(2,1)S(1)} %get-tuple-element.34), channel_id=1, source_target_pairs={{0,4},{4,0},{8,12},{12,8},{1,5},{5,1},{9,13},{13,9},{2,6},{6,2},{1... | collective-permute-start | bytes 835592 | tf_op jit(solution)/shard_map/ppermute | solution.py:596
  7.2 12.0 %collective-permute-start.1 = (s16[544,128]{1,0:T(8,128)(2,1)S(1)}, s16[544,128]{1,0:T(8,128)(2,1)S(1)}, u32[]{:S(2)}, u32[]{:S(2)}) collective-permute-start(s16[544,128]{1,0:T(8,128)(2,1)S(1)} %get-tuple-element.37), channel_id=1, source_target_pairs={{0,1},{1,0},{2,3},{3,2},{4,8},{5,9},{6,10},{7,11},{8,4},{9,5},{10,... | collective-permute-start | bytes 417800 | tf_op jit(solution)/shard_map/ppermute | solution.py:614
  7.3 11.9 %collective-permute-start.3 = (s16[272,128]{1,0:T(8,128)(2,1)S(1)}, s16[272,128]{1,0:T(8,128)(2,1)S(1)}, u32[]{:S(2)}, u32[]{:S(2)}) collective-permute-start(s16[272,128]{1,0:T(8,128)(2,1)S(1)} %get-tuple-element.38), channel_id=1, source_target_pairs={{0,12},{4,8},{8,4},{12,0},{1,13},{5,9},{9,5},{13,1},{2,14},{6,10},... | collective-permute-start | bytes 208904 | tf_op jit(solution)/shard_map/ppermute | solution.py:612
  9.8 9.4 %collective-permute-start.2 = (s16[272,128]{1,0:T(8,128)(2,1)S(1)}, s16[272,128]{1,0:T(8,128)(2,1)S(1)}, u32[]{:S(2)}, u32[]{:S(2)}) collective-permute-start(s16[272,128]{1,0:T(8,128)(2,1)S(1)} %get-tuple-element.38), channel_id=1, source_target_pairs={{0,8},{4,12},{8,0},{12,4},{1,9},{5,13},{9,1},{13,5},{2,10},{6,14},... | collective-permute-start | bytes 208904 | tf_op jit(solution)/shard_map/ppermute | solution.py:612

commit v5 on v4

--- a/solution.py
+++ b/solution.py
@@ -91,15 +91,21 @@
 
 
 class Pool:
-    def __init__(self, levels, tokens):
-        self.levels, self.tokens = levels, tokens
+    def __init__(self, levels, tokens, turned=False):
+        self.levels, self.tokens, self.turned = levels, tokens, turned
         self.whole = [level for level in levels if LEAF // 2**level % 16 == 0]
         parts = [pool_rows(2**level, 0, LEAF // 2**level) for level in self.whole]
         self.matrix = jnp.concatenate(parts, axis=0) if parts else None
         self.pieces, self.sums = {}, {}
 
     def add(self, leaf, values):
-        both = dot(self.matrix, values) if self.whole else None
+        if self.turned:
+            both = lax.dot_general(
+                self.matrix, values, (((1,), (1,)), ((), ())), preferred_element_type=F32
+            )
+            values = values.T
+        else:
+            both = dot(self.matrix, values) if self.whole else None
         at = 0
         for level in self.levels:
             block, first = place(level, leaf, self.tokens)
@@ -275,10 +281,9 @@
 
     def after(n):
         cols = slice(n * LEAF, (n + 1) * LEAF)
-        rows = got[n].T
-        kv_rows[cols, :] = rows
+        masked[n] = valid_only(got[n].T, counts[rank * leaves + n])
+        kv_rows[cols, :] = masked[n]
         v_cols[:, cols] = got[n][LANES:]
-        masked[n] = valid_only(rows, counts[rank * leaves + n])
 
     def halos():
         low, high = got[0].astype(F32), got[leaves - 1].astype(F32)
@@ -329,7 +334,7 @@
     leaves = tokens // LEAF
     first_leaf = rank * leaves
     near_terms = {}
-    q_pool = Pool((1, 2) + tuple(remote), tokens)
+    q_pool = Pool((1, 2) + tuple(remote), tokens, True)
     kv_pool = Pool((1, 2), tokens)
     for n in range(leaves):
         cols = slice(n * LEAF, (n + 1) * LEAF)
@@ -353,13 +358,14 @@
 
         return first, second
 
-    staggered([near_unit(n) for n in range(1, leaves - 1)])
     for n in range(leaves):
         cols = slice(n * LEAF, (n + 1) * LEAF)
-        q_pool.add(n, q_cols[:, cols].T)
+        q_pool.add(n, q_cols[:, cols])
     for n in range(leaves):
         cols = slice(n * LEAF, (n + 1) * LEAF)
-        kv_pool.add(n, valid_only(kv_rows[cols, :], counts[first_leaf + n]))
+        kv_pool.add(n, kv_rows[cols, :])
+
+    staggered([near_unit(n) for n in range(1, leaves - 1)])
 
     def queries(level, block):
         hi, lo = split(q_pool.get(level, block).T * (SCALE / 2**level))
@@ -435,68 +441,105 @@
             mass_out[index][:, i * rows : (i + 1) * rows] = mass(counts, start, leaves, group, rows)
 
 
+def end_unit(tokens, side, halo, q_cols, kv_rows, v_cols, end_marks, keep):
+    leaves = tokens // LEAF
+    keys, values = [x.astype(BF16) for x in halo]
+    inner = pl.ds(pl.multiple_of(side * ((leaves - 2) * LEAF), LEAF), 2 * LEAF)
+    own = pl.ds(pl.multiple_of(side * ((leaves - 1) * LEAF), LEAF), LEAF)
+
+    def first():
+        return near_scores(
+            jnp.concatenate([keys.T, kv_rows[inner, :][:, :LANES]], axis=0),
+            end_marks[side],
+            q_cols[:, own],
+        )
+
+    def second(scores):
+        window = jnp.concatenate([values, v_cols[:, inner]], axis=1)
+        for h in range(2):
+            keep(h, near(scores, window, h))
+
+    return first, second
+
+
+def far_units(tokens, level, fields, queries, mass_rows, keep):
+    means, sums = [jnp.concatenate(field, axis=1) for field in zip(*fields)]
+    keys = far_keys(means, mass_rows[...])
+    values = far_values(sums, mass_rows[...])
+    units = []
+    for h in range(2):
+
+        def second(scores, h=h):
+            keep(h, far(scores, values[h]))
+
+        units.append((functools.partial(far_scores, keys[h], queries[h]), second))
+    return units
+
+
+def pair_kernel(
+    tokens, level, q_cols, kv_rows, v_cols, end_marks, queries, mass_rows, pair,
+    far_out, far_stat, end_out, end_stat
+):
+    side = 1 - lax.axis_index("seq") % 2
+
+    def keeper(sums_ref, stat_ref):
+        def keep(h, term):
+            stat_ref[h, 0:1, :], sums_ref[h], stat_ref[h, 1:2, :] = term
+
+        return keep
+
+    rows = level_shape(level, tokens)[1]
+    units = far_units(
+        tokens, level, [decode(pair, halo_rows(), rows)], queries, mass_rows, keeper(far_out, far_stat)
+    )
+    units.append(
+        end_unit(
+            tokens, side, decode(pair, 0, LEAF), q_cols, kv_rows, v_cols, end_marks,
+            keeper(end_out, end_stat),
+        )
+    )
+    staggered(units, 2)
+
+
 def last_kernel(
     tokens, remote, q_cols, kv_rows, v_cols, sums_in, stat_in, end_marks, matrices, *rest
 ):
     levels = len(remote)
-    queries, mass_in = rest[:levels], rest[levels : 2 * levels]
-    pair, step = rest[2 * levels : 2 * levels + 2]
-    packs = rest[2 * levels + 2 : -3]
+    queries, mass_in = rest[: levels - 1], rest[levels - 1 : 2 * levels - 2]
+    far_in, far_stat, end_in, end_stat, step = rest[2 * levels - 2 : 2 * levels + 3]
+    packs = rest[2 * levels + 3 : -3]
     out, stage, sems = rest[-3:]
-    rank = lax.axis_index("seq")
+    odd = lax.axis_index("seq") % 2
     leaves = tokens // LEAF
-    flag = jnp.where(rank % 2 == 1, 1, 0)
+    results = {}
+    steps = {}
+    for h in range(2):
+        results[0, h] = (far_stat[h, 0:1, :], far_in[h], far_stat[h, 1:2, :])
+    units = []
+    for index in reversed(range(1, levels)):
+        rows = level_shape(remote[index], tokens)[1]
+        fields = [decode(packs[2**index - 2 + i], 0, rows) for i in range(2**index)]
+
+        def keep(h, term, index=index):
+            results[index, h] = term
+
+        units += far_units(
+            tokens, remote[index], fields, queries[index - 1], mass_in[index - 1], keep
+        )
+    units.append(
+        end_unit(
+            tokens, odd, decode(step, 0, LEAF), q_cols, kv_rows, v_cols, end_marks, steps.__setitem__
+        )
+    )
+    staggered(units, 2)
+    first_is_pair = jnp.where(odd == 1, 1, 0)
     ends = {}
-    results = {}
-
-    halo_pair = decode(pair, 0, LEAF)
-    halo_step = decode(step, 0, LEAF)
-
-    def near_unit(side):
-        own = flag if side == 0 else 1 - flag
-        inner = slice(side * (leaves - 2) * LEAF, (side * (leaves - 2) + 2) * LEAF)
-        keys, values = [
-            jnp.where(own == 1, here, there).astype(BF16)
-            for here, there in zip(halo_pair, halo_step)
-        ]
-
-        def first():
-            return near_scores(
-                jnp.concatenate([keys.T, kv_rows[inner, :LANES]], axis=0),
-                end_marks[side],
-                q_cols[:, side * (leaves - 1) * LEAF : (side * (leaves - 1) + 1) * LEAF],
+    for h in range(2):
+        pair_term = (end_stat[h, 0:1, :], end_in[h], end_stat[h, 1:2, :])
+        for n, flag in ((0, first_is_pair), (leaves - 1, 1 - first_is_pair)):
+            ends[n, h] = tuple(
+                jnp.where(flag == 1, x, y) for x, y in zip(pair_term, steps[h])
             )
-
-        def second(scores):
-            window = jnp.concatenate([values, v_cols[:, inner]], axis=1)
-            for h in range(2):
-                ends[side * (leaves - 1), h] = near(scores, window, h)
-
-        return first, second
-
-    def far_units(index):
-        level = remote[index]
-        group, rows, _ = level_shape(level, tokens)
-        if index == 0:
-            fields = [decode(pair, halo_rows(), rows)]
-        else:
-            fields = [decode(packs[2**index - 2 + i], 0, rows) for i in range(2**index)]
-        means, sums = [jnp.concatenate(field, axis=1) for field in zip(*fields)]
-        keys = far_keys(means, mass_in[index][...])
-        values = far_values(sums, mass_in[index][...])
-        units = []
-        for h in range(2):
-
-            def second(scores, h=h):
-                results[index, h] = far(scores, values[h])
-
-            units.append((functools.partial(far_scores, keys[h], queries[index][h]), second))
-        return units
-
-    units = []
-    for index in reversed(range(levels)):
-        units += far_units(index)
-    staggered(units + [near_unit(0), near_unit(1)], 2)
 
     coarse = []
     for h in range(2):
@@ -630,13 +673,27 @@
             pltpu.VMEM((tokens, LANES), BF16),
         ],
         compiler_params=params(),
-        cost_estimate=pl.CostEstimate(flops=2**20, bytes_accessed=2**16, transcendentals=0),
+        cost_estimate=pl.CostEstimate(flops=2**31, bytes_accessed=2**16, transcendentals=0),
         name="local_attention",
     )(counts, q.reshape(flat), order_here, kv_rows, v_cols)
+    sums, stat, end_marks, matrices = local[:4]
+    queries, masses = local[4 : 4 + len(remote)], local[4 + len(remote) :]
+    term = [shape((2, HEAD, LEAF), F32), shape((2, 2, LEAF), F32)]
+    paired = pl.pallas_call(
+        functools.partial(pair_kernel, tokens, remote[0]),
+        out_shape=term + term,
+        in_specs=[VMEM] * 7,
+        out_specs=[VMEM] * 4,
+        compiler_params=params(),
+        cost_estimate=pl.CostEstimate(flops=2**28, bytes_accessed=2**20, transcendentals=2**19),
+        name="pair_attention",
+    )(q_cols, kv_rows, v_cols, end_marks, queries[0], masses[0], got_pair)
+    last_args = [q_cols, kv_rows, v_cols, sums, stat, end_marks, matrices]
+    last_args += [*queries[1:], *masses[1:], *paired, got_step, *got]
     return pl.pallas_call(
         functools.partial(last_kernel, tokens, remote),
         out_shape=shape((2, HEAD, tokens), BF16),
-        in_specs=[VMEM] * (5 + len(local) + len(got)),
+        in_specs=[VMEM] * len(last_args),
         out_specs=ANY,
         scratch_shapes=[
             pltpu.VMEM((2, HEAD, tokens), BF16),
@@ -645,7 +702,7 @@
         compiler_params=params(),
         cost_estimate=pl.CostEstimate(flops=2**30, bytes_accessed=4 * 2**20, transcendentals=2**20),
         name="remote_attention",
-    )(q_cols, kv_rows, v_cols, *local, got_pair, got_step, *got)
+    )(*last_args)
 
 
 def shards(q, k, v, order, counts):

time: 22.2 us -> 20.8 us (0.937)
  starting transfers between devices: 7.76 us -> 5.82 us
  waiting for transfers between devices: 0.03 us -> 0.39 us
    ppermute x2, starting transfers between devices: 4.6 us -> 2.73 us  [head_pair(): lax.ppermute(packs[index - 1], 'seq', [(i, i ^ partner) for i in range(co...]
    pallas_call x0 -> x1, Pallas kernels: none -> 1.04 us  [head_pair(): pl.pallas_call(functools.partial(pair_kernel, tokens, remote[0]), out_sha...]
    pallas_call x1, Pallas kernels: 2.86 us -> 2.32 us  [head_pair(): pl.pallas_call(functools.partial(last_kernel, tokens, remote), out_shape=...]
    pallas_call x1, Pallas kernels: 7.29 us -> 6.9 us  [head_pair(): pl.pallas_call(functools.partial(local_kernel, tokens, remote), out_shape...]
    ppermute x2, waiting for transfers between devices: 0.03 us -> 0.39 us  [head_pair(): lax.ppermute(packs[index - 1], 'seq', [(i, i ^ partner) for i in range(co...]
  transfers between devices with their start and end apart: 4 -> 4, of which waited for: 0 -> 1; matrix products, arithmetic and copies ran while one was open for 0% -> 0% of each run, Pallas kernels for 33% -> 39%
where the time goes in v5:
time: 20.8 us; the launch traced here: 20.6 us
  Pallas kernels  14.4 us (69%)
  starting transfers between devices  5.82 us (28%)
  waiting for transfers between devices  0.39 us (2%)
    pallas_call x1, Pallas kernels, head_pair(): pl.pallas_call(functools.partial(local_kernel, tokens, remote), out_shape...  6.9 us
    pallas_call x1, Pallas kernels, head_pair(): pl.pallas_call(functools.partial(key_kernel, tokens, remote), out_shape=o...  4.02 us
    ppermute x1, starting transfers between devices, head_pair(): got_pair = lax.ppermute(pair, 'seq', [(i, i ^ 1) for i in range(count)])  3.09 us
    ppermute x2, starting transfers between devices, head_pair(): lax.ppermute(packs[index - 1], 'seq', [(i, i ^ partner) for i in range(co...  2.73 us
    pallas_call x1, Pallas kernels, head_pair(): pl.pallas_call(functools.partial(last_kernel, tokens, remote), out_shape=...  2.32 us
    pallas_call x1, Pallas kernels, head_pair(): pl.pallas_call(functools.partial(pair_kernel, tokens, remote[0]), out_sha...  1.04 us
  transfers between devices with their start and end apart: 4, of which 1 were waited for; matrix products, arithmetic and copies ran while one was open for 0% of the time, Pallas kernels for 39%

profile of v5, /device:TPU:0, one launch (start us, length us, event | category | flops | bytes accessed | tf_op | source)
XLA Modules:
  0.0 20.6 jit_solution(10641059010545414176)
XLA Ops:
  0.0 0.0 copy-start
  0.0 4.0 %gather_keys.1 = (bf16[2048,256]{1,0:T(8,128)(2,1)S(1)}, bf16[128,2048]{1,0:T(8,128)(2,1)S(1)}, s32[1,2048]{1,0:T(1,128)S(1)}, bf16[256,256]{1,0:T(8,128)(2,1)S(...) custom-call(s32[32]{0:T(128)} %counts_in.3, s32[1,2048]{1,0:T(1,128)} %order_in.1, bf16[128,2048]{1,0:T(8,128)(2,1)} %bitcast.4, ...), custom_call_target="tpu_custom_call" | custom-call | flops 2147483648 | bytes 4194304 | tf_op jit(solution)/shard_map/gather_keys/pallas_call | solution.py:622
  4.0 3.1 %collective-permute-start = (s16[1088,128]{1,0:T(8,128)(2,1)S(1)}, s16[1088,128]{1,0:T(8,128)(2,1)S(1)}, u32[]{:S(2)}, u32[]{:S(2)}) collective-permute-start(s16[1088,128]{1,0:T(8,128)(2,1)S(1)} %get-tuple-element.38), channel_id=1, source_target_pairs={{0,4},{4,0},{8,12},{12,8},{1,5},{5,1},{9,13},{13,9},{2,6},{6,2},{1... | collective-permute-start | bytes 835592 | tf_op jit(solution)/shard_map/ppermute | solution.py:639
  7.1 0.1 pack_rest.1
  7.2 2.5 %collective-permute-start.3 = (s16[272,128]{1,0:T(8,128)(2,1)S(1)}, s16[272,128]{1,0:T(8,128)(2,1)S(1)}, u32[]{:S(2)}, u32[]{:S(2)}) collective-permute-start(s16[272,128]{1,0:T(8,128)(2,1)S(1)} %get-tuple-element.46), channel_id=1, source_target_pairs={{0,12},{4,8},{8,4},{12,0},{1,13},{5,9},{9,5},{13,1},{2,14},{6,10},... | collective-permute-start | bytes 208904 | tf_op jit(solution)/shard_map/ppermute | solution.py:655
  9.7 0.2 collective-permute-start.2
  9.9 0.0 collective-permute-start.1
  9.9 0.0 copy-done
  9.9 6.9 %local_attention.1 = (bf16[128,2048]{1,0:T(8,128)(2,1)S(1)}, f32[2,64,2048]{2,1,0:T(8,128)S(1)}, f32[2,2,2048]{2,1,0:T(2,128)S(1)}, bf16[2,768,128]{2,1,0:T(8,12...) custom-call(s32[32]{0:T(128)} %counts_in.3, ...), custom_call_target="tpu_custom_call" | custom-call | flops 2147483648 | bytes 65536 | tf_op jit(solution)/shard_map/local_attention/pallas_call | solution.py:665
  16.9 0.0 collective-permute-done.pair
  16.9 1.0 %pair_attention.1 = (f32[2,64,256]{2,1,0:T(8,128)S(1)}, f32[2,2,256]{2,1,0:T(2,128)S(1)}, f32[2,64,256]{2,1,0:T(8,128)S(1)}, f32[2,2,256]{2,1,0:T(2,128)S(1)}) custom-call(bf16[128,2048]{1,0:T(8,128)(2,1)S(1)} %get-tuple-element.29.q_cols, bf16[2048,256]{1,0:T(8,128)(2,1)S(1)} %get-tuple-element.27.kv_rows, bf16[128,2048]{1,0:T(8,128)(2,1)S(1)} %get-tuple-element.28.v_cols, ...), custom_call_target="tpu_custom_call" | custom-call | flops 268435456 | bytes 1048576 | tf_op jit(solution)/shard_map/pair_attention/pallas_call | solution.py:682
  17.9 0.4 %collective-permute-done.3.rest_8_ = s16[272,128]{1,0:T(8,128)(2,1)S(1)} collective-permute-done((s16[272,128]{1,0:T(8,128)(2,1)S(1)}, s16[272,128]{1,0:T(8,128)(2,1)S(1)}, u32[]{:S(2)}, u32[]{:S(2)}) %collective-permute-start.3) | collective-permute-done | bytes 69664 | tf_op jit(solution)/shard_map/ppermute | solution.py:655
  18.3 0.0 collective-permute-done.2.rest_7_
  18.3 0.0 collective-permute-done.1.rest_6_
  18.3 2.3 %remote_attention.1 = bf16[2,64,2048]{2,1,0:T(8,128)(2,1)} custom-call(bf16[128,2048]{1,0:T(8,128)(2,1)S(1)} %get-tuple-element.29.q_cols, bf16[2048,256]{1,0:T(8,128)(2,1)S(1)} %get-tuple-element.27.kv_rows, bf16[128,2048]{1,0:T(8,128)(2,1)S(1)} %get-tuple-element.28.v_cols, f32[2,64,2048]{2,1,0:T(8,128)S(1)} %get-tuple-element.30.sums_in, ...), custom_call_target="tpu_custom_call" | custom-call | flops 1073741824 | bytes 4194304 | tf_op jit(solution)/shard_map/remote_attention/pallas_call | solution.py:693
Async XLA Ops:
  0.0 9.9 %copy-start = (bf16[2,64,2048]{2,1,0:T(8,128)(2,1)S(1)}, bf16[2,64,2048]{2,1,0:T(8,128)(2,1)}, u32[]{:S(2)}) copy-start(bf16[2,64,2048]{2,1,0:T(8,128)(2,1)} %param.5) | copy-start | bytes 1572868
  4.0 12.8 %collective-permute-start = (s16[1088,128]{1,0:T(8,128)(2,1)S(1)}, s16[1088,128]{1,0:T(8,128)(2,1)S(1)}, u32[]{:S(2)}, u32[]{:S(2)}) collective-permute-start(s16[1088,128]{1,0:T(8,128)(2,1)S(1)} %get-tuple-element.38), channel_id=1, source_target_pairs={{0,4},{4,0},{8,12},{12,8},{1,5},{5,1},{9,13},{13,9},{2,6},{6,2},{1... | collective-permute-start | bytes 835592 | tf_op jit(solution)/shard_map/ppermute | solution.py:639
  7.2 11.1 %collective-permute-start.3 = (s16[272,128]{1,0:T(8,128)(2,1)S(1)}, s16[272,128]{1,0:T(8,128)(2,1)S(1)}, u32[]{:S(2)}, u32[]{:S(2)}) collective-permute-start(s16[272,128]{1,0:T(8,128)(2,1)S(1)} %get-tuple-element.46), channel_id=1, source_target_pairs={{0,12},{4,8},{8,4},{12,0},{1,13},{5,9},{9,5},{13,1},{2,14},{6,10},... | collective-permute-start | bytes 208904 | tf_op jit(solution)/shard_map/ppermute | solution.py:655
  9.7 8.6 %collective-permute-start.2 = (s16[272,128]{1,0:T(8,128)(2,1)S(1)}, s16[272,128]{1,0:T(8,128)(2,1)S(1)}, u32[]{:S(2)}, u32[]{:S(2)}) collective-permute-start(s16[272,128]{1,0:T(8,128)(2,1)S(1)} %get-tuple-element.46), channel_id=1, source_target_pairs={{0,8},{4,12},{8,0},{12,4},{1,9},{5,13},{9,1},{13,5},{2,10},{6,14},... | collective-permute-start | bytes 208904 | tf_op jit(solution)/shard_map/ppermute | solution.py:655
  9.9 8.4 %collective-permute-start.1 = (s16[544,128]{1,0:T(8,128)(2,1)S(1)}, s16[544,128]{1,0:T(8,128)(2,1)S(1)}, u32[]{:S(2)}, u32[]{:S(2)}) collective-permute-start(s16[544,128]{1,0:T(8,128)(2,1)S(1)} %get-tuple-element.45), channel_id=1, source_target_pairs={{0,1},{1,0},{2,3},{3,2},{4,8},{5,9},{6,10},{7,11},{8,4},{9,5},{10,... | collective-permute-start | bytes 417800 | tf_op jit(solution)/shard_map/ppermute | solution.py:657

commit v6 on v5

--- a/solution.py
+++ b/solution.py
@@ -365,7 +365,6 @@
         cols = slice(n * LEAF, (n + 1) * LEAF)
         kv_pool.add(n, kv_rows[cols, :])
 
-    staggered([near_unit(n) for n in range(1, leaves - 1)])
 
     def queries(level, block):
         hi, lo = split(q_pool.get(level, block).T * (SCALE / 2**level))
@@ -391,6 +390,7 @@
                     results[at] = far(scores, value)
 
                 units.append((functools.partial(far_scores, keys[h], query[h]), second))
+    staggered([near_unit(n) for n in range(1, leaves - 1)])
     staggered(units, 4)
     for index, level in enumerate(remote):
         block = queries(level, 0)

time: 20.8 us -> 20.8 us (level)
  no operation moved by 1% of the time
where the time goes in v6:
time: 20.8 us; the launch traced here: 20.6 us
  Pallas kernels  14.4 us (69%)
  starting transfers between devices  5.82 us (28%)
  waiting for transfers between devices  0.39 us (2%)
    pallas_call x1, Pallas kernels, head_pair(): pl.pallas_call(functools.partial(local_kernel, tokens, remote), out_shape...  6.9 us
    pallas_call x1, Pallas kernels, head_pair(): pl.pallas_call(functools.partial(key_kernel, tokens, remote), out_shape=o...  4.02 us
    ppermute x1, starting transfers between devices, head_pair(): got_pair = lax.ppermute(pair, 'seq', [(i, i ^ 1) for i in range(count)])  3.09 us
    ppermute x2, starting transfers between devices, head_pair(): lax.ppermute(packs[index - 1], 'seq', [(i, i ^ partner) for i in range(co...  2.73 us
    pallas_call x1, Pallas kernels, head_pair(): pl.pallas_call(functools.partial(last_kernel, tokens, remote), out_shape=...  2.32 us
    pallas_call x1, Pallas kernels, head_pair(): pl.pallas_call(functools.partial(pair_kernel, tokens, remote[0]), out_sha...  1.04 us
  transfers between devices with their start and end apart: 4, of which 1 were waited for; matrix products, arithmetic and copies ran while one was open for 0% of the time, Pallas kernels for 39%

profile of v6, /device:TPU:0, one launch (start us, length us, event | category | flops | bytes accessed | tf_op | source)
XLA Modules:
  0.0 20.6 jit_solution(10641059010545414176)
XLA Ops:
  0.0 0.0 copy-start
  0.0 4.0 %gather_keys.1 = (bf16[2048,256]{1,0:T(8,128)(2,1)S(1)}, bf16[128,2048]{1,0:T(8,128)(2,1)S(1)}, s32[1,2048]{1,0:T(1,128)S(1)}, bf16[256,256]{1,0:T(8,128)(2,1)S(...) custom-call(s32[32]{0:T(128)} %counts_in.3, s32[1,2048]{1,0:T(1,128)} %order_in.1, bf16[128,2048]{1,0:T(8,128)(2,1)} %bitcast.4, ...), custom_call_target="tpu_custom_call" | custom-call | flops 2147483648 | bytes 4194304 | tf_op jit(solution)/shard_map/gather_keys/pallas_call | solution.py:622
  4.0 3.1 %collective-permute-start = (s16[1088,128]{1,0:T(8,128)(2,1)S(1)}, s16[1088,128]{1,0:T(8,128)(2,1)S(1)}, u32[]{:S(2)}, u32[]{:S(2)}) collective-permute-start(s16[1088,128]{1,0:T(8,128)(2,1)S(1)} %get-tuple-element.38), channel_id=1, source_target_pairs={{0,4},{4,0},{8,12},{12,8},{1,5},{5,1},{9,13},{13,9},{2,6},{6,2},{1... | collective-permute-start | bytes 835592 | tf_op jit(solution)/shard_map/ppermute | solution.py:639
  7.1 0.1 pack_rest.1
  7.2 2.5 %collective-permute-start.3 = (s16[272,128]{1,0:T(8,128)(2,1)S(1)}, s16[272,128]{1,0:T(8,128)(2,1)S(1)}, u32[]{:S(2)}, u32[]{:S(2)}) collective-permute-start(s16[272,128]{1,0:T(8,128)(2,1)S(1)} %get-tuple-element.46), channel_id=1, source_target_pairs={{0,12},{4,8},{8,4},{12,0},{1,13},{5,9},{9,5},{13,1},{2,14},{6,10},... | collective-permute-start | bytes 208904 | tf_op jit(solution)/shard_map/ppermute | solution.py:655
  9.7 0.2 collective-permute-start.2
  9.9 0.0 collective-permute-start.1
  9.9 0.0 copy-done
  9.9 6.9 %local_attention.1 = (bf16[128,2048]{1,0:T(8,128)(2,1)S(1)}, f32[2,64,2048]{2,1,0:T(8,128)S(1)}, f32[2,2,2048]{2,1,0:T(2,128)S(1)}, bf16[2,768,128]{2,1,0:T(8,12...) custom-call(s32[32]{0:T(128)} %counts_in.3, ...), custom_call_target="tpu_custom_call" | custom-call | flops 2147483648 | bytes 65536 | tf_op jit(solution)/shard_map/local_attention/pallas_call | solution.py:665
  16.9 0.0 collective-permute-done.pair
  16.9 1.0 %pair_attention.1 = (f32[2,64,256]{2,1,0:T(8,128)S(1)}, f32[2,2,256]{2,1,0:T(2,128)S(1)}, f32[2,64,256]{2,1,0:T(8,128)S(1)}, f32[2,2,256]{2,1,0:T(2,128)S(1)}) custom-call(bf16[128,2048]{1,0:T(8,128)(2,1)S(1)} %get-tuple-element.29.q_cols, bf16[2048,256]{1,0:T(8,128)(2,1)S(1)} %get-tuple-element.27.kv_rows, bf16[128,2048]{1,0:T(8,128)(2,1)S(1)} %get-tuple-element.28.v_cols, ...), custom_call_target="tpu_custom_call" | custom-call | flops 268435456 | bytes 1048576 | tf_op jit(solution)/shard_map/pair_attention/pallas_call | solution.py:682
  17.9 0.4 %collective-permute-done.3.rest_8_ = s16[272,128]{1,0:T(8,128)(2,1)S(1)} collective-permute-done((s16[272,128]{1,0:T(8,128)(2,1)S(1)}, s16[272,128]{1,0:T(8,128)(2,1)S(1)}, u32[]{:S(2)}, u32[]{:S(2)}) %collective-permute-start.3) | collective-permute-done | bytes 69664 | tf_op jit(solution)/shard_map/ppermute | solution.py:655
  18.3 0.0 collective-permute-done.2.rest_7_
  18.3 0.0 collective-permute-done.1.rest_6_
  18.3 2.3 %remote_attention.1 = bf16[2,64,2048]{2,1,0:T(8,128)(2,1)} custom-call(bf16[128,2048]{1,0:T(8,128)(2,1)S(1)} %get-tuple-element.29.q_cols, bf16[2048,256]{1,0:T(8,128)(2,1)S(1)} %get-tuple-element.27.kv_rows, bf16[128,2048]{1,0:T(8,128)(2,1)S(1)} %get-tuple-element.28.v_cols, f32[2,64,2048]{2,1,0:T(8,128)S(1)} %get-tuple-element.30.sums_in, ...), custom_call_target="tpu_custom_call" | custom-call | flops 1073741824 | bytes 4194304 | tf_op jit(solution)/shard_map/remote_attention/pallas_call | solution.py:693
Async XLA Ops:
  0.0 9.9 %copy-start = (bf16[2,64,2048]{2,1,0:T(8,128)(2,1)S(1)}, bf16[2,64,2048]{2,1,0:T(8,128)(2,1)}, u32[]{:S(2)}) copy-start(bf16[2,64,2048]{2,1,0:T(8,128)(2,1)} %param.5) | copy-start | bytes 1572868
  4.0 12.8 %collective-permute-start = (s16[1088,128]{1,0:T(8,128)(2,1)S(1)}, s16[1088,128]{1,0:T(8,128)(2,1)S(1)}, u32[]{:S(2)}, u32[]{:S(2)}) collective-permute-start(s16[1088,128]{1,0:T(8,128)(2,1)S(1)} %get-tuple-element.38), channel_id=1, source_target_pairs={{0,4},{4,0},{8,12},{12,8},{1,5},{5,1},{9,13},{13,9},{2,6},{6,2},{1... | collective-permute-start | bytes 835592 | tf_op jit(solution)/shard_map/ppermute | solution.py:639
  7.2 11.1 %collective-permute-start.3 = (s16[272,128]{1,0:T(8,128)(2,1)S(1)}, s16[272,128]{1,0:T(8,128)(2,1)S(1)}, u32[]{:S(2)}, u32[]{:S(2)}) collective-permute-start(s16[272,128]{1,0:T(8,128)(2,1)S(1)} %get-tuple-element.46), channel_id=1, source_target_pairs={{0,12},{4,8},{8,4},{12,0},{1,13},{5,9},{9,5},{13,1},{2,14},{6,10},... | collective-permute-start | bytes 208904 | tf_op jit(solution)/shard_map/ppermute | solution.py:655
  9.7 8.6 %collective-permute-start.2 = (s16[272,128]{1,0:T(8,128)(2,1)S(1)}, s16[272,128]{1,0:T(8,128)(2,1)S(1)}, u32[]{:S(2)}, u32[]{:S(2)}) collective-permute-start(s16[272,128]{1,0:T(8,128)(2,1)S(1)} %get-tuple-element.46), channel_id=1, source_target_pairs={{0,8},{4,12},{8,0},{12,4},{1,9},{5,13},{9,1},{13,5},{2,10},{6,14},... | collective-permute-start | bytes 208904 | tf_op jit(solution)/shard_map/ppermute | solution.py:655
  9.9 8.4 %collective-permute-start.1 = (s16[544,128]{1,0:T(8,128)(2,1)S(1)}, s16[544,128]{1,0:T(8,128)(2,1)S(1)}, u32[]{:S(2)}, u32[]{:S(2)}) collective-permute-start(s16[544,128]{1,0:T(8,128)(2,1)S(1)} %get-tuple-element.45), channel_id=1, source_target_pairs={{0,1},{1,0},{2,3},{3,2},{4,8},{5,9},{6,10},{7,11},{8,4},{9,5},{10,... | collective-permute-start | bytes 417800 | tf_op jit(solution)/shard_map/ppermute | solution.py:657
